TPU v7x, 32 devices: a whole 2x2x4 slice. The times are simulated.
32 devices in a mesh: groups: 2 (over y), sec: 4 (over z), term: 4 (over x, core).
Axes of the slice: x: 2, y: 2, z: 4, core: 2. Of those that a mesh axis runs over, the one named last changes fastest.
Arguments:
- psi: bfloat16 [64, 2, 16, 128, 128], P(('groups', 'sec')), parts along dimension 0, may hold values from -6 to 6
- left_env: bfloat16 [64, 16, 128, 128], P(('groups', 'sec'), 'term'), parts along dimension 0
- right_env: bfloat16 [64, 16, 128, 128], P(('groups', 'sec'), 'term'), parts along dimension 0
- local_ops: bfloat16 [8, 16, 16], replicated
- term_op: int32 [16], P('term'), may hold values from 0 to 7
- sector_rows: int32 [64], P('groups'), parts along dimension 0, may hold values from 64 to 128, as said below
- block_partner: int32 [64, 2], P(('groups', 'sec')), parts along dimension 0, may hold values from 0 to 31, as said below
- block_count: int32 [64], P(('groups', 'sec')), parts along dimension 0, may hold values from 1 to 2, as said below
Outputs:
- residual: bfloat16 [64, 2, 16, 128, 128], P(('groups', 'sec')), parts along dimension 0
- rayleigh: float32 [2], P('groups'), parts along dimension 0
There are 2 independent parts, one for each index of `groups`. A program takes and returns all parts, laid end to end along the dimension named above; an argument that names none is the same for every part. Nothing has to cross between parts.
Inputs may be any that keep to these rules, and one draw needn't show every extreme that they name: `sector_rows`: some sector has all 128 rows live. `block_partner`: the 2 partner sectors of one left sector are distinct. `block_count`: some sector has all 2 blocks live.
All inputs are finite; a program needn't handle non-finite values.
Results may differ from a plain program's by a relative error of at most 0.0045.
Values may be sent and summed in bfloat16 or wider, within the bound.
No kernel may reach another device: no remote copies, remote signals or barrier semaphores. Data moves between devices by JAX's collectives and lax.ppermute only.
A program may use at most 192 MiB of HBM per device.

v0:
```python
import functools

import jax
import jax.numpy as jnp
from jax import lax
from jax.experimental import pallas as pl
from jax.experimental.pallas import tpu as pltpu
from jax.sharding import PartitionSpec as P

TILE = 16
WIDE = 2
MIB = 1024 * 1024
SPARE = 4 * MIB
HASTE = 256


def block_facts(scalars, index, slot):
    meta, places, sector_rows, partners, counts = scalars
    sector = places[index]
    live = slot < counts[sector]
    own_rows = sector_rows[meta[0] + sector]
    partner_rows = sector_rows[partners[sector, slot]]
    return sector, live, own_rows, partner_rows


def live_entries(own_rows, partner_rows, width):
    left = lax.broadcasted_iota(jnp.int32, (1, width, width), 1) < own_rows
    right = lax.broadcasted_iota(jnp.int32, (1, width, width), 2) < partner_rows
    return left & right


def folded(values):
    states, width = values.shape[0], values.shape[-1]
    return jnp.sum(values.reshape(states * width // 8, 8, width), axis=0)


def by_live_rows(own_rows, groups, work):
    always = groups // 2
    work(0, always)
    for group in range(always, groups, WIDE):
        pl.when(own_rows > group * TILE)(functools.partial(work, group, group + WIDE))


def spread_operators(ops_ref, chosen, spread_ops, at, states):
    width, wide = ops_ref.shape[-1], states * TILE
    row_state = lax.broadcasted_iota(jnp.int32, (wide, states), 0) // TILE
    column = lax.broadcasted_iota(jnp.int32, (wide, states), 1)
    pick_rows = (row_state == column).astype(jnp.bfloat16)
    row = lax.broadcasted_iota(jnp.int32, (width, wide), 0)
    column_state = lax.broadcasted_iota(jnp.int32, (width, wide), 1) // TILE
    pick_columns = (row == column_state).astype(jnp.bfloat16)
    inner_row = lax.rem(lax.broadcasted_iota(jnp.int32, (wide, wide), 0), TILE)
    inner_column = lax.rem(lax.broadcasted_iota(jnp.int32, (wide, wide), 1), TILE)
    for term in chosen:
        operator = ops_ref[term * states : (term + 1) * states, :]
        rows = jnp.dot(pick_rows, operator, preferred_element_type=jnp.float32)
        full = jnp.dot(
            rows.astype(jnp.bfloat16), pick_columns, preferred_element_type=jnp.float32
        )
        spread_ops[at] = jnp.where(inner_row == inner_column, full, 0.0).astype(jnp.bfloat16)
        at += 1


def multiply_left(lefts, live_psi, after_left):
    terms, groups = after_left.shape[:2]
    states, width = live_psi.shape[0], live_psi.shape[-1]
    for pair in range(states // WIDE):
        columns = jnp.concatenate([live_psi[pair * WIDE + at] for at in range(WIDE)], axis=1)
        done = jnp.dot(lefts, columns, preferred_element_type=jnp.float32).astype(jnp.bfloat16)
        for term in range(terms):
            for at in range(WIDE):
                state = pair * WIDE + at
                after_left[term, :, state * TILE : (state + 1) * TILE, :] = done[
                    term * width : (term + 1) * width, at * width : (at + 1) * width
                ].reshape(groups, TILE, width)


def apply_operators(low, high, spread_ops, after_left, targets):
    width = after_left.shape[-1]
    for group in range(low, high, WIDE):
        for term, (target, lead) in enumerate(targets):
            columns = jnp.concatenate(
                [after_left[term, group + at] for at in range(WIDE)], axis=1
            )
            done = jnp.dot(
                spread_ops[term], columns, preferred_element_type=jnp.float32
            ).astype(jnp.bfloat16)
            for at in range(WIDE):
                target[(*lead, group + at)] = done[:, at * width : (at + 1) * width]


def each_live_block(half, slots, scalars, work):
    meta = scalars[0]

    def visit(block, carry):
        place, slot = block // slots, lax.rem(block, slots)
        sector, live, own_rows, partner_rows = block_facts(
            scalars, meta[1] * half + place, slot
        )
        pl.when(live)(functools.partial(work, block, place, sector, own_rows, partner_rows))
        return carry

    lax.fori_loop(0, half * slots, visit, 0)


def pack_kernel(chunks, half, terms, places, term_op, ops_ref, left_ref, right_ref, *rest):
    payloads, rest = rest[:2], rest[2:]
    shares, sems = rest[: len(chunks)], rest[len(chunks)]
    states, width = ops_ref.shape[1], left_ref.shape[-1]
    copied = half * terms * width
    for part, payload in enumerate(payloads):
        for place in range(half):
            pltpu.make_async_copy(
                left_ref.at[places[part * half + place]],
                payload.at[pl.ds(place * terms * width, terms * width)],
                sems.at[part],
            ).start()
    moves = []
    for at, (start, length) in enumerate(chunks):
        move = pltpu.make_async_copy(
            right_ref.at[:, pl.ds(start, length)], shares[at], sems.at[2 + at]
        )
        move.start()
        moves.append(move)
    for payload in payloads:
        for term in range(terms):
            rows = slice(copied + term * states, copied + (term + 1) * states)
            payload[rows, :] = jnp.zeros((states, width), jnp.bfloat16)
            payload[rows, :states] = ops_ref[term_op[term]]
    for part, payload in enumerate(payloads):
        whole = payload.at[pl.ds(0, copied)]
        pltpu.make_async_copy(whole, whole, sems.at[part]).wait()
    for move in moves:
        move.wait()


def pack_call(chunks, places, term_op, local_ops, left_env, right_env):
    sectors, terms, width = left_env.shape[:3]
    half, states = sectors // 2, local_ops.shape[1]
    payload = jax.ShapeDtypeStruct((terms * (half * width + states), width), jnp.bfloat16)
    shares = [
        jax.ShapeDtypeStruct((sectors, length, width, width), jnp.bfloat16)
        for start, length in chunks
    ]
    return pl.pallas_call(
        functools.partial(pack_kernel, chunks, half, terms),
        in_specs=in_smem(2) + resident(1) + [pl.BlockSpec(memory_space=pltpu.HBM)] * 2,
        out_specs=resident(2 + len(chunks)),
        out_shape=[payload, payload] + shares,
        scratch_shapes=[pltpu.SemaphoreType.DMA((2 + len(chunks),))],
        compiler_params=pltpu.CompilerParams(vmem_limit_bytes=58 * MIB),
        cost_estimate=pl.CostEstimate(
            flops=0, bytes_accessed=4 * left_env.size, transcendentals=0
        ),
        name="pack",
    )(places, term_op, local_ops, left_env.reshape(sectors, terms * width, width), right_env)


def source_views(payloads):
    views = []
    for payload in payloads:
        views += [payload] if len(payload.shape) == 2 else [payload.at[0], payload.at[1]]
    return views


def term_rows(place, held, start, terms, width):
    return pl.ds(pl.multiple_of((place * held + start) * width, width), terms * width)


def left_kernel(first, held, items, count, afters, half, slots, meta, places, sector_rows,
                partners, counts, *rest):
    scalars = (meta, places, sector_rows, partners, counts)
    psi_ref, rest = rest[afters], rest[afters + 1 :]
    payloads, rest = rest[:count], rest[count:]
    outs, rest = rest[: len(items)], rest[len(items) :]
    token_ref, rest = rest[0], rest[1:]
    if first:
        live_psi, square_ref, spread_ops, after_left, sems = rest
    else:
        live_psi = psi_ref
        spread_ops, after_left = rest
    states, width = live_psi.shape[1], live_psi.shape[-1]
    views = source_views(payloads)

    def fetch(block, sector):
        return pltpu.make_async_copy(
            psi_ref.at[sector, lax.rem(block, slots)], live_psi.at[block], sems.at[block]
        )

    if first:
        each_live_block(
            half, slots, scalars, lambda block, place, sector, *rows: fetch(block, sector).start()
        )
        square_ref[...] = jnp.zeros_like(square_ref)
    at = 0
    for source, start, terms in items:
        operators = views[source][half * held * width :, :]
        spread_operators(operators, range(start, start + terms), spread_ops, at, states)
        at += terms
    token_ref[...] = jnp.zeros_like(token_ref)

    def work(block, place, sector, own_rows, partner_rows):
        if first:
            fetch(block, sector).wait()
            mask = live_entries(own_rows, partner_rows, width)
            kept = jnp.where(mask, live_psi[block], jnp.zeros((), jnp.bfloat16))
            live_psi[block] = kept
            wide_psi = kept.astype(jnp.float32)
            square_ref[...] += folded(wide_psi * wide_psi)
        lefts = [
            views[source][term_rows(place, held, start, terms, width), :]
            for source, start, terms in items
        ]
        multiply_left(jnp.concatenate(lefts, axis=0), live_psi.at[block], after_left)
        targets = [
            (outs[at], (block, term))
            for at, (source, start, terms) in enumerate(items)
            for term in range(terms)
        ]
        by_live_rows(
            own_rows,
            width // TILE,
            lambda low, high: apply_operators(low, high, spread_ops, after_left, targets),
        )

    each_live_block(half, slots, scalars, work)


def resident(count):
    return [pl.BlockSpec(memory_space=pltpu.VMEM)] * count


def in_smem(count):
    return [pl.BlockSpec(memory_space=pltpu.SMEM)] * count


def left_call(first, scalars, held, items, shape, psi, payloads, afters):
    blocks, slots, states, width = shape
    groups, wide = width // TILE, states * TILE
    every = sum(terms for source, start, terms in items)
    fold_shape = jax.ShapeDtypeStruct((8, width), jnp.float32)
    out_shape = [
        jax.ShapeDtypeStruct((blocks, terms, groups, wide, width), jnp.bfloat16)
        for source, start, terms in items
    ] + [fold_shape]
    scratch = [
        pltpu.VMEM((every, wide, wide), jnp.bfloat16),
        pltpu.VMEM((every, groups, wide, width), jnp.bfloat16),
    ]
    if first:
        live_psi = jax.ShapeDtypeStruct((blocks, states, width, width), jnp.bfloat16)
        out_shape += [live_psi, fold_shape]
        scratch.append(pltpu.SemaphoreType.DMA((blocks,)))
    psi_spec = [pl.BlockSpec(memory_space=pltpu.HBM)] if first else resident(1)
    return pl.pallas_call(
        functools.partial(
            left_kernel, first, held, items, len(payloads), len(afters), blocks // slots, slots
        ),
        in_specs=in_smem(len(scalars))
        + [pl.BlockSpec(memory_space=pl.ANY)] * len(afters)
        + psi_spec
        + resident(len(payloads)),
        out_specs=resident(len(out_shape)),
        out_shape=out_shape,
        scratch_shapes=scratch,
        compiler_params=pltpu.CompilerParams(
            vmem_limit_bytes=max(
                28 * MIB if first else 0,
                SPARE + 2 * every * (wide * wide + groups * wide * width),
            )
        ),
        cost_estimate=pl.CostEstimate(
            flops=psi.size * every * (width + wide) // HASTE,
            bytes_accessed=psi.size // HASTE,
            transcendentals=0,
        ),
        name="left",
    )(*scalars, *afters, psi, *payloads)


def choose_kernel(devices, afters, sectors, half, slots, meta, places, partners, *rest):
    rest = rest[afters:]
    shards, (mine_ref, other_ref) = rest[:devices], rest[devices:]
    for part, out_ref in enumerate((mine_ref, other_ref)):
        for block in range(half * slots):
            sector = places[(meta[1] ^ part) * half + block // slots]
            partner = partners[sector, block % slots]
            away = lax.rem(meta[3] + devices - partner // sectors, devices)
            place = lax.rem(partner, sectors)
            for distance in range(devices):
                @pl.when(away == distance)
                def _(distance=distance, place=place, block=block, out_ref=out_ref):
                    out_ref[block] = shards[distance][place]


def choose_call(scalars, half, slots, shards, afters):
    meta, places, _, partners, _ = scalars
    sectors, terms, width = shards[0].shape[:3]
    chosen = jax.ShapeDtypeStruct((half * slots, terms, width, width), jnp.bfloat16)
    return pl.pallas_call(
        functools.partial(choose_kernel, len(shards), len(afters), sectors, half, slots),
        in_specs=in_smem(3)
        + [pl.BlockSpec(memory_space=pl.ANY)] * len(afters)
        + resident(len(shards)),
        out_specs=resident(2),
        out_shape=[chosen, chosen],
        compiler_params=pltpu.CompilerParams(vmem_limit_bytes=SPARE),
        cost_estimate=pl.CostEstimate(
            flops=0, bytes_accessed=8 * half * slots * terms * width * width, transcendentals=0
        ),
        name="choose",
    )(meta, places, partners, *afters, *shards)


def chunk_kernel(first, last, held, chunk, ahead, late, count, half, slots,
                 meta, places, sector_rows, partners, counts, after_ref, psi_ref, *rest):
    start, terms = chunk
    early_refs, rest = rest[: len(ahead)], rest[len(ahead) :]
    payloads, rest = rest[:count], rest[count:]
    near_rights, rest = rest[:2], rest[2:]
    devices = len(ahead) + len(late)
    far_rights, rest = rest[: devices // 2 - 1], rest[devices // 2 - 1 :]
    if not first:
        sum_in, rest = rest[0], rest[1:]
    sum_out, fold_ref, *rest = rest
    if late:
        spread_ops, after_left, after_ops, *rest = rest
    states, width = psi_ref.shape[1], psi_ref.shape[-1]
    groups = width // TILE
    views = dict(zip(late, source_views(payloads)))
    rights = list(near_rights) + [right.at[side] for right in far_rights for side in (0, 1)]
    for at, source in enumerate(late):
        operators = views[source][half * held * width :, :]
        spread_operators(operators, range(start, start + terms), spread_ops, at * terms, states)
    fold_ref[...] = jnp.zeros_like(fold_ref)
    if last:
        sum_out[...] = jnp.zeros_like(sum_out)

    def work(block, place, sector, own_rows, partner_rows):
        total = rest[0] if last else sum_out.at[block]
        if late:
            lefts = [
                views[source][term_rows(place, held, start, terms, width), :] for source in late
            ]
            multiply_left(jnp.concatenate(lefts, axis=0), psi_ref.at[block], after_left)
        columns = [
            jnp.concatenate(
                [rights[pair + at][block, term] for at in range(2) for term in range(terms)],
                axis=0,
            )
            for pair in range(0, devices, 2)
        ]

        def operated(device, term, group):
            if device in ahead:
                return early_refs[ahead.index(device)][block, term, group]
            return after_ops[late.index(device) * terms + term, group]

        def multiply(low, high):
            if late:
                targets = [(after_ops, (term,)) for term in range(len(late) * terms)]
                apply_operators(low, high, spread_ops, after_left, targets)
            for group in range(low, high, WIDE):
                parts = []
                for pair in range(0, devices, 2):
                    rows = jnp.concatenate(
                        [
                            jnp.concatenate(
                                [
                                    operated(pair + at, term, group + side)
                                    for at in range(2)
                                    for term in range(terms)
                                ],
                                axis=1,
                            )
                            for side in range(WIDE)
                        ],
                        axis=0,
                    )
                    parts.append(
                        jnp.dot(rows, columns[pair // 2], preferred_element_type=jnp.float32)
                    )
                while len(parts) > 1:
                    parts = [parts[at] + parts[at + 1] for at in range(0, len(parts), 2)]
                done = parts[0].reshape(WIDE, states, TILE, width)
                for side in range(WIDE):
                    tile = slice((group + side) * TILE, (group + side + 1) * TILE)
                    if first:
                        total[:, tile, :] = done[side]
                    else:
                        total[:, tile, :] = sum_in[block, :, tile, :] + done[side]

        by_live_rows(own_rows, groups, multiply)
        if last:
            mask = live_entries(own_rows, partner_rows, width)
            kept = jnp.where(mask, total[...], 0.0)
            fold_ref[...] += folded(kept * psi_ref[block].astype(jnp.float32))
            sum_out[block] = kept.astype(jnp.bfloat16)

    each_live_block(half, slots, (meta, places, sector_rows, partners, counts), work)


def chunk_call(first, last, held, chunk, ahead, late, scalars, slots, psi, early, payloads,
               rights, total, after):
    blocks, states, width = psi.shape[:3]
    groups, wide = width // TILE, states * TILE
    start, terms = chunk
    operands = [after, psi, *early, *payloads, *rights]
    aliases = {}
    if not first:
        operands.append(total)
        if not last:
            aliases = {len(scalars) + len(operands) - 1: 0}
    sum_dtype = jnp.bfloat16 if last else jnp.float32
    every = len(late) * terms
    scratch = []
    if late:
        scratch += [
            pltpu.VMEM((every, wide, wide), jnp.bfloat16),
            pltpu.VMEM((every, groups, wide, width), jnp.bfloat16),
            pltpu.VMEM((every, groups, wide, width), jnp.bfloat16),
        ]
    if last:
        scratch.append(pltpu.VMEM((states, width, width), jnp.float32))
    work = psi.size * terms * ((len(ahead) + len(late)) * width + len(late) * (width + wide))
    return pl.pallas_call(
        functools.partial(
            chunk_kernel, first, last, held, chunk, ahead, late, len(payloads),
            blocks // slots, slots,
        ),
        in_specs=in_smem(len(scalars))
        + [pl.BlockSpec(memory_space=pl.ANY)]
        + resident(len(operands) - 1),
        out_specs=resident(2),
        out_shape=[
            jax.ShapeDtypeStruct(psi.shape, sum_dtype),
            jax.ShapeDtypeStruct((8, width), jnp.float32),
        ],
        scratch_shapes=scratch,
        input_output_aliases=aliases,
        compiler_params=pltpu.CompilerParams(
            vmem_limit_bytes=SPARE + 2 * every * wide * (wide + 2 * groups * width)
        ),
        cost_estimate=pl.CostEstimate(
            flops=work // HASTE, bytes_accessed=psi.size // HASTE, transcendentals=0
        ),
        name="chunk",
    )(*scalars, *operands)


def residual_kernel(half, slots, meta, places, sector_rows, partners, counts,
                    folds_ref, live_psi, own_ref, other_ref, psi_ref, out_ref, quotient_ref,
                    other_psi, staged, read_sems, write_sems):
    scalars = (meta, places, sector_rows, partners, counts)
    blocks, width = own_ref.shape[0], own_ref.shape[-1]
    depth = staged.shape[0]

    def where(block, side):
        index = (meta[1] ^ side) * half + block // slots
        return places[index], block % slots, index

    def read(block):
        sector, slot, _ = where(block, 1)
        return pltpu.make_async_copy(
            psi_ref.at[sector, slot], other_psi.at[block], read_sems.at[block]
        )

    def write(step):
        sector, slot, _ = where(step % blocks, step // blocks)
        return pltpu.make_async_copy(
            staged.at[step % depth], out_ref.at[sector, slot], write_sems.at[step % depth]
        )

    for block in range(blocks):
        read(block).start()
    quotient = jnp.sum(folds_ref[0:8, :]) / jnp.sum(folds_ref[8:16, :])
    quotient_ref[0] = quotient
    for step in range(2 * blocks):
        block, side = step % blocks, step // blocks
        if step >= depth:
            write(step - depth).wait()
        sector, slot, index = where(block, side)
        _, live, own_rows, partner_rows = block_facts(scalars, index, slot)
        mask = live_entries(jnp.where(live, own_rows, 0), partner_rows, width)
        if side:
            read(block).wait()
            values, sums = other_psi[block], other_ref[block]
        else:
            values, sums = live_psi[block], own_ref[block]
        scaled = quotient * jnp.where(mask, values.astype(jnp.float32), 0.0)
        staged[step % depth] = (sums.astype(jnp.float32) - scaled).astype(jnp.bfloat16)
        write(step).start()
    for step in range(2 * blocks - min(depth, 2 * blocks), 2 * blocks):
        write(step).wait()


def residual_call(scalars, folds, psi, live_psi, own, other):
    sectors, slots, states, width = psi.shape[:4]
    blocks = own.shape[0]
    depth = 4
    in_hbm = [pl.BlockSpec(memory_space=pltpu.HBM)]
    return pl.pallas_call(
        functools.partial(residual_kernel, sectors // 2, slots),
        in_specs=in_smem(len(scalars)) + resident(4) + in_hbm,
        out_specs=in_hbm + in_smem(1),
        out_shape=[
            jax.ShapeDtypeStruct(psi.shape, jnp.bfloat16),
            jax.ShapeDtypeStruct((1,), jnp.float32),
        ],
        scratch_shapes=[
            pltpu.VMEM((blocks, states, width, width), jnp.bfloat16),
            pltpu.VMEM((depth, states, width, width), jnp.bfloat16),
            pltpu.SemaphoreType.DMA((blocks,)),
            pltpu.SemaphoreType.DMA((depth,)),
        ],
        compiler_params=pltpu.CompilerParams(vmem_limit_bytes=41 * MIB),
        cost_estimate=pl.CostEstimate(
            flops=3 * psi.size, bytes_accessed=6 * psi.size, transcendentals=0
        ),
        name="residual",
    )(*scalars, folds, live_psi, own, other, psi)


def on_device(
    devices, rings, psi, left_env, right_env, local_ops, term_op, sector_rows, block_partner,
    block_count,
):
    sectors, slots, states, width = psi.shape[:4]
    terms = left_env.shape[1]
    half = sectors // 2
    me = lax.axis_index("term")
    ring = lax.axis_index("sec")
    core = me % 2
    meta = jnp.stack([ring * sectors, core, me, ring]).astype(jnp.int32)

    near_rows = lax.dynamic_slice_in_dim(sector_rows, ring * sectors, sectors)
    weight = block_count * (near_rows + width // 2)
    order = jnp.arange(sectors, dtype=jnp.int32)
    ahead = (weight[None, :] > weight[:, None]) | (
        (weight[None, :] == weight[:, None]) & (order[None, :] < order[:, None])
    )
    rank = jnp.sum(ahead.astype(jnp.int32), axis=1)
    index = ((rank ^ (rank >> 1)) & 1) * half + (rank >> 1)
    places = jnp.sum(jnp.where(index[None, :] == order[:, None], order[None, :], 0), axis=1)
    scalars = (meta, places, sector_rows, block_partner, block_count)

    def swap(value, bits, axis="term", size=devices):
        return lax.ppermute(value, axis, [(i, i ^ bits) for i in range(size)])

    def to_far_chips(near, received):
        both = jnp.stack([near, received])
        return both, [swap(both, bits) for bits in range(2, devices, 2)]

    chunks = [(0, terms // 2)] + [(at, 1) for at in range(terms // 2, terms)]
    ordered = jnp.roll(places, -core * half)
    mine, theirs, *shares = pack_call(
        chunks, ordered, term_op, local_ops, left_env, right_env
    )
    near_left = swap(theirs, 1)
    both_lefts, far_lefts = to_far_chips(mine, near_left)

    shards, rights = [], []

    def gather(token):
        own = shares[len(shards)]
        if token is not None:
            own, _ = lax.optimization_barrier((own, token))
        moved = [own]
        for distance in range(1, rings):
            pairs = [(i, (i + distance) % rings) for i in range(rings)]
            moved.append(lax.ppermute(own, "sec", pairs))
        shards.append(moved)

    def choose(token):
        afters = [token] + (rights[-1][2:] if rights else [])
        mine, other = choose_call(scalars, half, slots, shards[len(rights)], afters)
        received = swap(other, 1)
        both, far_rights = to_far_chips(mine, received)
        rights.append([mine, received] + far_rights)
        return both

    products = {}
    shape = (half * slots, slots, states, width)
    far = tuple(range(2, devices))

    def go_left(sources, which, token, first=False, waits=()):
        items = [(source, *chunks[at]) for at in which for source in sources]
        near = [source for source in sources if source < 2]
        payloads = [(mine, near_left)[source] for source in near]
        if len(near) < len(sources):
            payloads += far_lefts
        renamed = [(sources.index(source), start, count) for source, start, count in items]
        outs = left_call(
            first, scalars, terms, renamed, shape, psi if first else live_psi, payloads,
            [token, *waits],
        )
        for at, out in zip([(at, source) for at in which for source in sources], outs):
            products[at] = out
        return outs[len(items) :]

    every = range(len(chunks))
    gather(None)
    token, live_psi, squares = go_left((0,), every, both_lefts, True)
    token, = go_left((1,), every, token, waits=far_lefts)
    gather(token)
    token = choose(token)
    total = None
    for at, chunk in enumerate(chunks):
        last = at == len(chunks) - 1
        if at == len(chunks) - 2:
            token, = go_left(far, [len(chunks) - 1], token)
        if len(rights) < len(chunks):
            token = choose(token)
        if len(shards) < len(chunks):
            gather(token)
        ahead = tuple(source for source in range(devices) if (at, source) in products)
        late = tuple(source for source in range(devices) if source not in ahead)
        total, token = chunk_call(
            at == 0, last, terms, chunk, ahead, late, scalars, slots, live_psi,
            [products.pop((at, source)) for source in ahead], far_lefts if late else [],
            rights[at], total, token,
        )

    other = swap(total, 1)
    folds = jnp.concatenate([token, squares], axis=0)
    bits = 1
    while bits < rings:
        folds = folds + swap(folds, bits, "sec", rings)
        bits *= 2
    folds = folds + swap(folds, 1)
    residual, rayleigh = residual_call(scalars, folds, psi, live_psi, total, other)
    return residual, rayleigh


def solution(mesh):
    placed = (
        P(("groups", "sec"), None, None, None, None),
        P(("groups", "sec"), "term", None, None),
        P(("groups", "sec"), "term", None, None),
        P(),
        P("term"),
        P("groups"),
        P(("groups", "sec"), None),
        P(("groups", "sec")),
    )
    return jax.shard_map(
        functools.partial(on_device, mesh.shape["term"], mesh.shape["sec"]),
        mesh=mesh,
        in_specs=placed,
        out_specs=(P(("groups", "sec"), None, None, None, None), P("groups")),
        check_vma=False,
    )
```

profile of v0, /device:TPU:5, one launch (start us, length us, event | category | flops | bytes accessed | tf_op | source)
XLA Modules:
  0.0 183.2 jit_solution(15892535764942199964)
XLA Ops:
  2.5 3.7 %pack.1 = (bf16[2112,128]{1,0:T(8,128)(2,1)}, bf16[2112,128]{1,0:T(8,128)(2,1)}, bf16[8,2,128,128]{3,2,1,0:T(8,128)(2,1)}, bf16[8,1,128,128]{3,2,1,0:T(8,128)(2,1)}, bf16[8,1,128,128]{3,2,1,0:T(8,128)(2,1)}) custom-call(s32[8]{0:T(128)} %dynamic_slice.8.places, s32[4]{0:T(128)} %term_op.1, bf16[8,16,16]{2,1,0:T(8,128)(2,1)} %ops_ref.1, ...), custom_call_target="tpu_custom_call" | custom-call | bytes 2097152 | tf_op jit(solution)/shard_map/pack/pallas_call | solution.py:145
  7.0 1.8 collective-permute-done.rest_3_
  11.2 3.3 %collective-permute-start.4 = (bf16[8,2,128,128]{3,2,1,0:T(8,128)(2,1)}, bf16[8,2,128,128]{3,2,1,0:T(8,128)(2,1)S(1)}, u32[]{:S(2)}, u32[]{:S(2)}) collective-permute-start(bf16[8,2,128,128]{3,2,1,0:T(8,128)(2,1)} %get-tuple-element.39.rest_1_), channel_id=1, source_target_pairs={{0,12},{4,0},{8,4},{12,8},{1,13},{5,1},{9,5},{13,9},{2,14},{6,2},{... | collective-permute-start | bytes 1572872 | tf_op jit(solution)/shard_map/ppermute | solution.py:571
  16.2 9.7 %left.3 = (bf16[8,2,8,256,128]{4,3,2,1,0:T(8,128)(2,1)S(1)}, bf16[8,1,8,256,128]{4,3,2,1,0:T(8,128)(2,1)S(1)}, bf16[8,1,8,256,128]{4,3,2,1,0:T(8,128)(2,1)S(1)},...) custom-call(s32[4]{0:T(128)S(1)} %pad_add_fusion.meta, ...), custom_call_target="tpu_custom_call" | custom-call | flops 25165824 | bytes 16384 | tf_op jit(solution)/shard_map/left/pallas_call | solution.py:255
  25.9 2.0 %copy-done.4 = bf16[8,1,8,256,128]{4,3,2,1,0:T(8,128)(2,1)} copy-done((bf16[8,1,8,256,128]{4,3,2,1,0:T(8,128)(2,1)}, bf16[8,1,8,256,128]{4,3,2,1,0:T(8,128)(2,1)S(1)}, u32[]{:S(2)}) %copy-start.4) | copy-done | bytes 4194328
  27.9 1.9 %copy-done.8 = bf16[8,1,8,256,128]{4,3,2,1,0:T(8,128)(2,1)} copy-done((bf16[8,1,8,256,128]{4,3,2,1,0:T(8,128)(2,1)}, bf16[8,1,8,256,128]{4,3,2,1,0:T(8,128)(2,1)S(1)}, u32[]{:S(2)}) %copy-start.8) | copy-done | bytes 4194328
  29.9 5.2 %collective-permute-done.1.rest_1_.rest_2_ = bf16[2,2112,128]{2,1,0:T(8,128)(2,1)S(1)} collective-permute-done((bf16[2,2112,128]{2,1,0:T(8,128)(2,1)S(1)}, bf16[2,2112,128]{2,1,0:T(8,128)(2,1)S(1)}, u32[]{:S(2)}, u32[]{:S(2)}) %collective-permute-start.1) | collective-permute-done | bytes 1081376 | tf_op jit(solution)/shard_map/ppermute | solution.py:548
  35.1 8.7 %left.4 = (bf16[8,2,8,256,128]{4,3,2,1,0:T(8,128)(2,1)S(1)}, bf16[8,1,8,256,128]{4,3,2,1,0:T(8,128)(2,1)S(1)}, bf16[8,1,8,256,128]{4,3,2,1,0:T(8,128)(2,1)S(1)}, f32[8,128]{1,0:T(8,128)S(1)}) custom-call(s32[4]{0:T(128)S(1)} %pad_add_fusion.meta, s32[8]{0:T(128)S(1)} %select_reduce_fusion.places, s32[32]{0:T(128)S(1)} %copy-done.21, ...), custom_call_target="tpu_custom_call" | custom-call | flops 12582912 | bytes 8192 | tf_op jit(solution)/shard_map/left/pallas_call | solution.py:255
  43.8 3.3 %copy-done.2 = bf16[8,2,8,256,128]{4,3,2,1,0:T(8,128)(2,1)} copy-done((bf16[8,2,8,256,128]{4,3,2,1,0:T(8,128)(2,1)}, bf16[8,2,8,256,128]{4,3,2,1,0:T(8,128)(2,1)S(1)}, u32[]{:S(2)}) %copy-start.2) | copy-done | bytes 8388632
  47.1 2.0 %copy-done.6 = bf16[8,1,8,256,128]{4,3,2,1,0:T(8,128)(2,1)} copy-done((bf16[8,1,8,256,128]{4,3,2,1,0:T(8,128)(2,1)}, bf16[8,1,8,256,128]{4,3,2,1,0:T(8,128)(2,1)S(1)}, u32[]{:S(2)}) %copy-start.6) | copy-done | bytes 4194328
  49.1 9.9 %collective-permute-done.3.rest_3_ = bf16[8,2,128,128]{3,2,1,0:T(8,128)(2,1)} collective-permute-done((bf16[8,2,128,128]{3,2,1,0:T(8,128)(2,1)}, bf16[8,2,128,128]{3,2,1,0:T(8,128)(2,1)}, u32[]{:S(2)}, u32[]{:S(2)}) %collective-permute-start.3) | collective-permute-done | bytes 524320 | tf_op jit(solution)/shard_map/ppermute | solution.py:571
  59.1 2.1 %choose.3 = (bf16[8,2,128,128]{3,2,1,0:T(8,128)(2,1)S(1)}, bf16[8,2,128,128]{3,2,1,0:T(8,128)(2,1)S(1)}) custom-call(s32[4]{0:T(128)S(1)} %pad_add_fusion.meta, s32[8]{0:T(128)S(1)} %select_reduce_fusion.places, s32[8,2]{1,0:T(8,128)S(1)} %copy.38.partners, f32[8,128]{1,0:T(8,128)S(1)} %get-tuple-element.38.rest_0_, bf16[8,2,128,128]{3,2,1,0:T(8,128)(2,1)S(1)} %copy-done.17, ...), custom_call_target="tpu_custom_call" | custom-call | bytes 2097152 | tf_op jit(solution)/shard_map/choose/pallas_call | solution.py:300
  61.1 1.6 collective-permute-start.5
  62.7 1.5 collective-permute-done.5.rest_4_
  64.7 2.5 %collective-permute-start.8 = (bf16[8,1,128,128]{3,2,1,0:T(8,128)(2,1)S(1)}, bf16[8,1,128,128]{3,2,1,0:T(8,128)(2,1)S(1)}, u32[]{:S(2)}, u32[]{:S(2)}) collective-permute-start(bf16[8,1,128,128]{3,2,1,0:T(8,128)(2,1)S(1)} %copy-done.18), channel_id=1, source_target_pairs={{0,8},{4,12},{8,0},{12,4},{1,9},{5,13},{9,1},{13,5},{2,10},{6,14},... | collective-permute-start | bytes 786440 | tf_op jit(solution)/shard_map/ppermute | solution.py:571
  68.7 3.2 %collective-permute-done.9.rest_5_ = bf16[8,1,128,128]{3,2,1,0:T(8,128)(2,1)S(1)} collective-permute-done((bf16[8,1,128,128]{3,2,1,0:T(8,128)(2,1)S(1)}, bf16[8,1,128,128]{3,2,1,0:T(8,128)(2,1)S(1)}, u32[]{:S(2)}, u32[]{:S(2)}) %collective-permute-start.9) | collective-permute-done | bytes 262176 | tf_op jit(solution)/shard_map/ppermute | solution.py:571
  71.9 18.2 %collective-permute-done.8.rest_4_ = bf16[8,1,128,128]{3,2,1,0:T(8,128)(2,1)S(1)} collective-permute-done((bf16[8,1,128,128]{3,2,1,0:T(8,128)(2,1)S(1)}, bf16[8,1,128,128]{3,2,1,0:T(8,128)(2,1)S(1)}, u32[]{:S(2)}, u32[]{:S(2)}) %collective-permute-start.8) | collective-permute-done | bytes 262176 | tf_op jit(solution)/shard_map/ppermute | solution.py:571
  96.9 3.4 %copy-done.1 = bf16[8,2,8,256,128]{4,3,2,1,0:T(8,128)(2,1)S(1)} copy-done((bf16[8,2,8,256,128]{4,3,2,1,0:T(8,128)(2,1)S(1)}, bf16[8,2,8,256,128]{4,3,2,1,0:T(8,128)(2,1)}, u32[]{:S(2)}) %copy-start.1) | copy-done | bytes 8388632
  100.3 13.8 %chunk.3 = (f32[8,16,128,128]{3,2,1,0:T(8,128)S(1)}, f32[8,128]{1,0:T(8,128)S(1)}) custom-call(s32[4]{0:T(128)S(1)} %pad_add_fusion.meta, s32[8]{0:T(128)S(1)} %select_reduce_fusion.places, s32[32]{0:T(128)S(1)} %copy-done.21, s32[8,2]{1,0:T(8,128)S(1)} %copy.38.partners, s32[8]{0:T(128)S(1)} %copy-done.20, ...), custom_call_target="tpu_custom_call" | custom-call | flops 20971520 | bytes 8192 | tf_op jit(solution)/shard_map/chunk/pallas_call | solution.py:426
  114.1 6.2 %left.5 = (bf16[8,1,8,256,128]{4,3,2,1,0:T(8,128)(2,1)S(1)}, bf16[8,1,8,256,128]{4,3,2,1,0:T(8,128)(2,1)S(1)}, f32[8,128]{1,0:T(8,128)S(1)}) custom-call(s32[4]{0:T(128)S(1)} %pad_add_fusion.meta, s32[8]{0:T(128)S(1)} %select_reduce_fusion.places, s32[32]{0:T(128)S(1)} %copy-done.21, s32[8,2]{1,0:T(8,128)S(1)} %copy.38.partners, s32[8]{0:T(128)S(1)} %copy-done.20, ...), custom_call_target="tpu_custom_call" | custom-call | flops 6291456 | bytes 8192 | tf_op jit(solution)/shard_map/left/pallas_call | solution.py:255
  120.3 2.0 %copy-done.12 = bf16[8,1,8,256,128]{4,3,2,1,0:T(8,128)(2,1)} copy-done((bf16[8,1,8,256,128]{4,3,2,1,0:T(8,128)(2,1)}, bf16[8,1,8,256,128]{4,3,2,1,0:T(8,128)(2,1)S(1)}, u32[]{:S(2)}) %copy-start.12) | copy-done | bytes 4194328
  122.3 2.0 %copy-done.14 = bf16[8,1,8,256,128]{4,3,2,1,0:T(8,128)(2,1)} copy-done((bf16[8,1,8,256,128]{4,3,2,1,0:T(8,128)(2,1)}, bf16[8,1,8,256,128]{4,3,2,1,0:T(8,128)(2,1)S(1)}, u32[]{:S(2)}) %copy-start.14) | copy-done | bytes 4194328
  125.8 2.4 %collective-permute-start.15 = (bf16[8,1,128,128]{3,2,0,1:T(8,128)(2,1)S(1)}, bf16[8,1,128,128]{3,2,0,1:T(8,128)(2,1)S(1)}, u32[]{:S(2)}, u32[]{:S(2)}) collective-permute-start(bf16[8,1,128,128]{3,2,0,1:T(8,128)(2,1)S(1)} %bitcast.28), channel_id=1, source_target_pairs={{0,1},{1,0},{2,3},{3,2},{4,5},{5,4},{6,7},{7,6},{8,9},{9,8},{10,11... | collective-permute-start | bytes 786440 | tf_op jit(solution)/shard_map/ppermute | solution.py:548
  130.7 9.6 %chunk.4 = (f32[8,16,128,128]{3,2,1,0:T(8,128)S(1)}, f32[8,128]{1,0:T(8,128)S(1)}) custom-call(s32[4]{0:T(128)S(1)} %pad_add_fusion.meta, s32[8]{0:T(128)S(1)} %select_reduce_fusion.places, s32[32]{0:T(128)S(1)} %copy-done.21, s32[8,2]{1,0:T(8,128)S(1)} %copy.38.partners, s32[8]{0:T(128)S(1)} %copy-done.20, ...), custom_call_target="tpu_custom_call", output_to_operand_aliasing={{0}: (13, {})} | custom-call | flops 10485760 | bytes 8192 | tf_op jit(solution)/shard_map/chunk/pallas_call | solution.py:426
  140.3 2.2 %collective-permute-done.16.rest_6_ = bf16[2,8,1,128,128]{4,3,2,1,0:T(8,128)(2,1)S(1)} collective-permute-done((bf16[2,8,1,128,128]{4,3,2,1,0:T(8,128)(2,1)S(1)}, bf16[2,8,1,128,128]{4,3,2,1,0:T(8,128)(2,1)S(1)}, u32[]{:S(2)}, u32[]{:S(2)}) %collective-permute-start.16) | collective-permute-done | bytes 524320 | tf_op jit(solution)/shard_map/ppermute | solution.py:548
  142.6 2.2 %copy-done.15 = bf16[8,1,8,256,128]{4,3,2,1,0:T(8,128)(2,1)S(1)} copy-done((bf16[8,1,8,256,128]{4,3,2,1,0:T(8,128)(2,1)S(1)}, bf16[8,1,8,256,128]{4,3,2,1,0:T(8,128)(2,1)}, u32[]{:S(2)}) %copy-start.15) | copy-done | bytes 4194328
  144.8 7.4 %chunk.5 = (bf16[8,16,128,128]{3,2,1,0:T(8,128)(2,1)S(1)}, f32[8,128]{1,0:T(8,128)S(1)}) custom-call(s32[4]{0:T(128)S(1)} %pad_add_fusion.meta, s32[8]{0:T(128)S(1)} %select_reduce_fusion.places, s32[32]{0:T(128)S(1)} %copy-done.21, s32[8,2]{1,0:T(8,128)S(1)} %copy.38.partners, s32[8]{0:T(128)S(1)} %copy-done.20, f32[8,128]{1,0:T(8,128)S(1)} %get-tuple-element.57.after_ref, ...), custom_call_target="tpu_custom_call" | custom-call | flops 4194304 | bytes 8192 | tf_op jit(solution)/shard_map/chunk/pallas_call | solution.py:426
  152.2 1.6 collective-permute-start.20
  153.7 2.5 %collective-permute-start.17 = (f32[16,128]{1,0:T(8,128)S(1)}, f32[16,128]{1,0:T(8,128)S(1)}, u32[]{:S(2)}, u32[]{:S(2)}) collective-permute-start(f32[16,128]{1,0:T(8,128)S(1)} %constant_dynamic-update-slice_fusion), channel_id=1, source_target_pairs={{0,4},{4,0},{8,12},{12,8},{1,5},{5,1},{9,13},{13,9},{2,6},{6,2},{1... | collective-permute-start | bytes 24584 | tf_op jit(solution)/shard_map/ppermute | solution.py:548
  157.3 15.1 %collective-permute-start.18 = (f32[16,128]{1,0:T(8,128)S(1)}, f32[16,128]{1,0:T(8,128)S(1)}, u32[]{:S(2)}, u32[]{:S(2)}) collective-permute-start(f32[16,128]{1,0:T(8,128)S(1)} %add.42), channel_id=1, source_target_pairs={{0,8},{4,12},{8,0},{12,4},{1,9},{5,13},{9,1},{13,5},{2,10},{6,14},... | collective-permute-start | bytes 24584 | tf_op jit(solution)/shard_map/ppermute | solution.py:548
  173.5 2.1 %collective-permute-start.19 = (f32[16,128]{1,0:T(8,128)S(1)}, f32[16,128]{1,0:T(8,128)S(1)}, u32[]{:S(2)}, u32[]{:S(2)}) collective-permute-start(f32[16,128]{1,0:T(8,128)S(1)} %add.43), channel_id=1, source_target_pairs={{0,1},{1,0},{2,3},{3,2},{4,5},{5,4},{6,7},{7,6},{8,9},{9,8},{10,11... | collective-permute-start | bytes 24584 | tf_op jit(solution)/shard_map/ppermute | solution.py:548
  176.5 6.6 %residual.1 = (bf16[8,2,16,128,128]{4,3,2,1,0:T(8,128)(2,1)}, f32[1]{0:T(128)}) custom-call(s32[4]{0:T(128)S(1)} %pad_add_fusion.meta, s32[8]{0:T(128)S(1)} %select_reduce_fusion.places, s32[32]{0:T(128)S(1)} %copy-done.21, s32[8,2]{1,0:T(8,128)S(1)} %copy.38.partners, s32[8]{0:T(128)S(1)} %copy-done.20, f32[16,128]{1,0:T(8,128)S(1)} %add.44.folds_ref, ...), custom_call_target="tpu_custom_call" | custom-call | flops 12582912 | bytes 25165824 | tf_op jit(solution)/shard_map/residual/pallas_call | solution.py:502
  (84 shorter events, 22.2 us)
Async XLA Ops:
  0.6 14.5 %copy-start.20 = (s32[8]{0:T(128)S(1)}, s32[8]{0:T(128)}, u32[]{:S(2)}) copy-start(s32[8]{0:T(128)} %counts.13) | copy-start | bytes 100
  0.6 14.5 %copy-start.21 = (s32[32]{0:T(128)S(1)}, s32[32]{0:T(128)}, u32[]{:S(2)}) copy-start(s32[32]{0:T(128)} %sector_rows.13) | copy-start | bytes 388
  0.7 14.3 %copy-start.22 = (s32[8,2]{0,1:T(2,128)S(1)}, s32[8,2]{0,1:T(2,128)}, u32[]{:S(2)}) copy-start(s32[8,2]{0,1:T(2,128)} %param.14) | copy-start | bytes 196
  6.3 2.5 %collective-permute-start = (bf16[2112,128]{1,0:T(8,128)(2,1)}, bf16[2112,128]{1,0:T(8,128)(2,1)S(1)}, u32[]{:S(2)}, u32[]{:S(2)}) collective-permute-start(bf16[2112,128]{1,0:T(8,128)(2,1)} %get-tuple-element.35), channel_id=1, source_target_pairs={{0,1},{1,0},{2,3},{3,2},{4,5},{5,4},{6,7},{7,6},{8,9},{9,8},{10,11... | collective-permute-start | bytes 1622024 | tf_op jit(solution)/shard_map/ppermute | solution.py:548
  9.9 25.1 %collective-permute-start.1 = (bf16[2,2112,128]{2,1,0:T(8,128)(2,1)S(1)}, bf16[2,2112,128]{2,1,0:T(8,128)(2,1)S(1)}, u32[]{:S(2)}, u32[]{:S(2)}) collective-permute-start(bf16[2,2112,128]{2,1,0:T(8,128)(2,1)S(1)} %pad_maximum_fusion.rest_0_), channel_id=1, source_target_pairs={{0,2},{1,3},{2,0},{3,1},{4,6},{5,7},{6,4},{7,5},{8,10},{9,11},{10,... | collective-permute-start | bytes 3244040 | tf_op jit(solution)/shard_map/ppermute | solution.py:548
  11.2 37.9 %collective-permute-start.4 = (bf16[8,2,128,128]{3,2,1,0:T(8,128)(2,1)}, bf16[8,2,128,128]{3,2,1,0:T(8,128)(2,1)S(1)}, u32[]{:S(2)}, u32[]{:S(2)}) collective-permute-start(bf16[8,2,128,128]{3,2,1,0:T(8,128)(2,1)} %get-tuple-element.39.rest_1_), channel_id=1, source_target_pairs={{0,12},{4,0},{8,4},{12,8},{1,13},{5,1},{9,5},{13,9},{2,14},{6,2},{... | collective-permute-start | bytes 1572872 | tf_op jit(solution)/shard_map/ppermute | solution.py:571
  14.5 44.5 %collective-permute-start.3 = (bf16[8,2,128,128]{3,2,1,0:T(8,128)(2,1)}, bf16[8,2,128,128]{3,2,1,0:T(8,128)(2,1)}, u32[]{:S(2)}, u32[]{:S(2)}) collective-permute-start(bf16[8,2,128,128]{3,2,1,0:T(8,128)(2,1)} %get-tuple-element.39.rest_1_), channel_id=1, source_target_pairs={{0,8},{4,12},{8,0},{12,4},{1,9},{5,13},{9,1},{13,5},{2,10},{6,14},... | collective-permute-start | bytes 1572872 | tf_op jit(solution)/shard_map/ppermute | solution.py:571
  14.5 44.5 %collective-permute-start.2 = (bf16[8,2,128,128]{3,2,1,0:T(8,128)(2,1)}, bf16[8,2,128,128]{3,2,1,0:T(8,128)(2,1)}, u32[]{:S(2)}, u32[]{:S(2)}) collective-permute-start(bf16[8,2,128,128]{3,2,1,0:T(8,128)(2,1)} %get-tuple-element.39.rest_1_), channel_id=1, source_target_pairs={{0,4},{4,8},{8,12},{12,0},{1,5},{5,9},{9,13},{13,1},{2,6},{6,10},{... | collective-permute-start | bytes 1572872 | tf_op jit(solution)/shard_map/ppermute | solution.py:571
  29.9 34.5 %copy-start = (bf16[8,2,8,256,128]{4,3,2,1,0:T(8,128)(2,1)}, bf16[8,2,8,256,128]{4,3,2,1,0:T(8,128)(2,1)S(1)}, u32[]{:S(2)}) copy-start(bf16[8,2,8,256,128]{4,3,2,1,0:T(8,128)(2,1)S(1)} %get-tuple-element.46.rest_0_) | copy-start | bytes 25165828
  29.9 29.2 %copy-start.17 = (bf16[8,2,128,128]{3,2,1,0:T(8,128)(2,1)S(1)}, bf16[8,2,128,128]{3,2,1,0:T(8,128)(2,1)}, u32[]{:S(2)}) copy-start(bf16[8,2,128,128]{3,2,1,0:T(8,128)(2,1)} %get-tuple-element.39.rest_1_) | copy-start | bytes 1572868
  35.1 29.6 %copy-start.18 = (bf16[8,1,128,128]{3,2,1,0:T(8,128)(2,1)S(1)}, bf16[8,1,128,128]{3,2,1,0:T(8,128)(2,1)}, u32[]{:S(2)}) copy-start(bf16[8,1,128,128]{3,2,1,0:T(8,128)(2,1)} %get-tuple-element.43.rest_2_) | copy-start | bytes 786436
  35.1 60.1 %copy-start.19 = (bf16[8,1,128,128]{3,2,1,0:T(8,128)(2,1)S(1)}, bf16[8,1,128,128]{3,2,1,0:T(8,128)(2,1)}, u32[]{:S(2)}) copy-start(bf16[8,1,128,128]{3,2,1,0:T(8,128)(2,1)} %get-tuple-element.51.rest_2_) | copy-start | bytes 786436
  49.1 44.7 %copy-start.10 = (bf16[8,1,8,256,128]{4,3,2,1,0:T(8,128)(2,1)}, bf16[8,1,8,256,128]{4,3,2,1,0:T(8,128)(2,1)S(1)}, u32[]{:S(2)}) copy-start(bf16[8,1,8,256,128]{4,3,2,1,0:T(8,128)(2,1)S(1)} %get-tuple-element.59.rest_1_) | copy-start | bytes 12582916
  59.1 37.8 %copy-start.3 = (bf16[8,2,8,256,128]{4,3,2,1,0:T(8,128)(2,1)S(1)}, bf16[8,2,8,256,128]{4,3,2,1,0:T(8,128)(2,1)}, u32[]{:S(2)}) copy-start(bf16[8,2,8,256,128]{4,3,2,1,0:T(8,128)(2,1)} %copy-done.2) | copy-start | bytes 25165828
  61.1 3.1 %collective-permute-start.5 = (bf16[8,2,128,128]{3,2,1,0:T(8,128)(2,1)S(1)}, bf16[8,2,128,128]{3,2,1,0:T(8,128)(2,1)S(1)}, u32[]{:S(2)}, u32[]{:S(2)}) collective-permute-start(bf16[8,2,128,128]{3,2,1,0:T(8,128)(2,1)S(1)} %get-tuple-element.41), channel_id=1, source_target_pairs={{0,1},{1,0},{2,3},{3,2},{4,5},{5,4},{6,7},{7,6},{8,9},{9,8},{10,11... | collective-permute-start | bytes 1572872 | tf_op jit(solution)/shard_map/ppermute | solution.py:548
  64.4 25.8 %collective-permute-start.6 = (bf16[2,8,2,128,128]{4,3,2,1,0:T(8,128)(2,1)S(1)}, bf16[2,8,2,128,128]{4,3,2,1,0:T(8,128)(2,1)S(1)}, u32[]{:S(2)}, u32[]{:S(2)}) collective-permute-start(bf16[2,8,2,128,128]{4,3,2,1,0:T(8,128)(2,1)S(1)} %pad_maximum_fusion.1.rest_0_), channel_id=1, source_target_pairs={{0,2},{1,3},{2,0},{3,1},{4,6},{5,7},{6,4},{7,5},{8,10},{9,11},{10,... | collective-permute-start | bytes 3145736 | tf_op jit(solution)/shard_map/ppermute | solution.py:548
  64.7 7.2 %collective-permute-start.9 = (bf16[8,1,128,128]{3,2,1,0:T(8,128)(2,1)S(1)}, bf16[8,1,128,128]{3,2,1,0:T(8,128)(2,1)S(1)}, u32[]{:S(2)}, u32[]{:S(2)}) collective-permute-start(bf16[8,1,128,128]{3,2,1,0:T(8,128)(2,1)S(1)} %copy-done.18), channel_id=1, source_target_pairs={{0,12},{4,0},{8,4},{12,8},{1,13},{5,1},{9,5},{13,9},{2,14},{6,2},{... | collective-permute-start | bytes 786440 | tf_op jit(solution)/shard_map/ppermute | solution.py:571
  64.7 25.4 %collective-permute-start.8 = (bf16[8,1,128,128]{3,2,1,0:T(8,128)(2,1)S(1)}, bf16[8,1,128,128]{3,2,1,0:T(8,128)(2,1)S(1)}, u32[]{:S(2)}, u32[]{:S(2)}) collective-permute-start(bf16[8,1,128,128]{3,2,1,0:T(8,128)(2,1)S(1)} %copy-done.18), channel_id=1, source_target_pairs={{0,8},{4,12},{8,0},{12,4},{1,9},{5,13},{9,1},{13,5},{2,10},{6,14},... | collective-permute-start | bytes 786440 | tf_op jit(solution)/shard_map/ppermute | solution.py:571
  67.2 22.9 %collective-permute-start.7 = (bf16[8,1,128,128]{3,2,1,0:T(8,128)(2,1)S(1)}, bf16[8,1,128,128]{3,2,1,0:T(8,128)(2,1)S(1)}, u32[]{:S(2)}, u32[]{:S(2)}) collective-permute-start(bf16[8,1,128,128]{3,2,1,0:T(8,128)(2,1)S(1)} %copy-done.18), channel_id=1, source_target_pairs={{0,4},{4,8},{8,12},{12,0},{1,5},{5,9},{9,13},{13,1},{2,6},{6,10},{... | collective-permute-start | bytes 786440 | tf_op jit(solution)/shard_map/ppermute | solution.py:571
  91.4 2.4 %collective-permute-start.10 = (bf16[8,1,128,128]{3,2,0,1:T(8,128)(2,1)S(1)}, bf16[8,1,128,128]{3,2,0,1:T(8,128)(2,1)S(1)}, u32[]{:S(2)}, u32[]{:S(2)}) collective-permute-start(bf16[8,1,128,128]{3,2,0,1:T(8,128)(2,1)S(1)} %bitcast.27), channel_id=1, source_target_pairs={{0,1},{1,0},{2,3},{3,2},{4,5},{5,4},{6,7},{7,6},{8,9},{9,8},{10,11... | collective-permute-start | bytes 786440 | tf_op jit(solution)/shard_map/ppermute | solution.py:548
  93.9 30.4 %collective-permute-start.11 = (bf16[2,8,1,128,128]{4,3,2,1,0:T(8,128)(2,1)S(1)}, bf16[2,8,1,128,128]{4,3,2,1,0:T(8,128)(2,1)S(1)}, u32[]{:S(2)}, u32[]{:S(2)}) collective-permute-start(bf16[2,8,1,128,128]{4,3,2,1,0:T(8,128)(2,1)S(1)} %pad_maximum_fusion.2.after_ref), channel_id=1, source_target_pairs={{0,2},{1,3},{2,0},{3,1},{4,6},{5,7},{6,4},{7,5},{8,10},{9,11},{10,... | collective-permute-start | bytes 1572872 | tf_op jit(solution)/shard_map/ppermute | solution.py:548
  95.2 29.1 %collective-permute-start.14 = (bf16[8,1,128,128]{3,2,1,0:T(8,128)(2,1)S(1)}, bf16[8,1,128,128]{3,2,1,0:T(8,128)(2,1)S(1)}, u32[]{:S(2)}, u32[]{:S(2)}) collective-permute-start(bf16[8,1,128,128]{3,2,1,0:T(8,128)(2,1)S(1)} %copy-done.19), channel_id=1, source_target_pairs={{0,12},{4,0},{8,4},{12,8},{1,13},{5,1},{9,5},{13,9},{2,14},{6,2},{... | collective-permute-start | bytes 786440 | tf_op jit(solution)/shard_map/ppermute | solution.py:571
  95.2 29.1 %collective-permute-start.13 = (bf16[8,1,128,128]{3,2,1,0:T(8,128)(2,1)S(1)}, bf16[8,1,128,128]{3,2,1,0:T(8,128)(2,1)S(1)}, u32[]{:S(2)}, u32[]{:S(2)}) collective-permute-start(bf16[8,1,128,128]{3,2,1,0:T(8,128)(2,1)S(1)} %copy-done.19), channel_id=1, source_target_pairs={{0,8},{4,12},{8,0},{12,4},{1,9},{5,13},{9,1},{13,5},{2,10},{6,14},... | collective-permute-start | bytes 786440 | tf_op jit(solution)/shard_map/ppermute | solution.py:571
  95.4 28.9 %collective-permute-start.12 = (bf16[8,1,128,128]{3,2,1,0:T(8,128)(2,1)S(1)}, bf16[8,1,128,128]{3,2,1,0:T(8,128)(2,1)S(1)}, u32[]{:S(2)}, u32[]{:S(2)}) collective-permute-start(bf16[8,1,128,128]{3,2,1,0:T(8,128)(2,1)S(1)} %copy-done.19), channel_id=1, source_target_pairs={{0,4},{4,8},{8,12},{12,0},{1,5},{5,9},{9,13},{13,1},{2,6},{6,10},{... | collective-permute-start | bytes 786440 | tf_op jit(solution)/shard_map/ppermute | solution.py:571
  100.3 30.4 %copy-start.7 = (bf16[8,1,8,256,128]{4,3,2,1,0:T(8,128)(2,1)S(1)}, bf16[8,1,8,256,128]{4,3,2,1,0:T(8,128)(2,1)}, u32[]{:S(2)}) copy-start(bf16[8,1,8,256,128]{4,3,2,1,0:T(8,128)(2,1)} %copy-done.6) | copy-start | bytes 12582916
  114.1 16.6 %copy-start.5 = (bf16[8,1,8,256,128]{4,3,2,1,0:T(8,128)(2,1)S(1)}, bf16[8,1,8,256,128]{4,3,2,1,0:T(8,128)(2,1)}, u32[]{:S(2)}) copy-start(bf16[8,1,8,256,128]{4,3,2,1,0:T(8,128)(2,1)} %copy-done.4) | copy-start | bytes 12582916
  125.8 3.5 %collective-permute-start.15 = (bf16[8,1,128,128]{3,2,0,1:T(8,128)(2,1)S(1)}, bf16[8,1,128,128]{3,2,0,1:T(8,128)(2,1)S(1)}, u32[]{:S(2)}, u32[]{:S(2)}) collective-permute-start(bf16[8,1,128,128]{3,2,0,1:T(8,128)(2,1)S(1)} %bitcast.28), channel_id=1, source_target_pairs={{0,1},{1,0},{2,3},{3,2},{4,5},{5,4},{6,7},{7,6},{8,9},{9,8},{10,11... | collective-permute-start | bytes 786440 | tf_op jit(solution)/shard_map/ppermute | solution.py:548
  129.4 13.2 %collective-permute-start.16 = (bf16[2,8,1,128,128]{4,3,2,1,0:T(8,128)(2,1)S(1)}, bf16[2,8,1,128,128]{4,3,2,1,0:T(8,128)(2,1)S(1)}, u32[]{:S(2)}, u32[]{:S(2)}) collective-permute-start(bf16[2,8,1,128,128]{4,3,2,1,0:T(8,128)(2,1)S(1)} %pad_maximum_fusion.3.after_ref), channel_id=1, source_target_pairs={{0,2},{1,3},{2,0},{3,1},{4,6},{5,7},{6,4},{7,5},{8,10},{9,11},{10,... | collective-permute-start | bytes 1572872 | tf_op jit(solution)/shard_map/ppermute | solution.py:548
  152.2 24.3 %collective-permute-start.20 = (bf16[8,16,128,128]{3,2,1,0:T(8,128)(2,1)S(1)}, bf16[8,16,128,128]{3,2,1,0:T(8,128)(2,1)S(1)}, u32[]{:S(2)}, u32[]{:S(2)}) collective-permute-start(bf16[8,16,128,128]{3,2,1,0:T(8,128)(2,1)S(1)} %get-tuple-element.65.own_ref), channel_id=1, source_target_pairs={{0,1},{1,0},{2,3},{3,2},{4,5},{5,4},{6,7},{7,6},{8,9},{9,8},{10,11... | collective-permute-start | bytes 12582920 | tf_op jit(solution)/shard_map/ppermute | solution.py:548
  153.7 3.6 %collective-permute-start.17 = (f32[16,128]{1,0:T(8,128)S(1)}, f32[16,128]{1,0:T(8,128)S(1)}, u32[]{:S(2)}, u32[]{:S(2)}) collective-permute-start(f32[16,128]{1,0:T(8,128)S(1)} %constant_dynamic-update-slice_fusion), channel_id=1, source_target_pairs={{0,4},{4,0},{8,12},{12,8},{1,5},{5,1},{9,13},{13,9},{2,6},{6,2},{1... | collective-permute-start | bytes 24584 | tf_op jit(solution)/shard_map/ppermute | solution.py:548
  157.3 16.2 %collective-permute-start.18 = (f32[16,128]{1,0:T(8,128)S(1)}, f32[16,128]{1,0:T(8,128)S(1)}, u32[]{:S(2)}, u32[]{:S(2)}) collective-permute-start(f32[16,128]{1,0:T(8,128)S(1)} %add.42), channel_id=1, source_target_pairs={{0,8},{4,12},{8,0},{12,4},{1,9},{5,13},{9,1},{13,5},{2,10},{6,14},... | collective-permute-start | bytes 24584 | tf_op jit(solution)/shard_map/ppermute | solution.py:548
  173.5 3.0 %collective-permute-start.19 = (f32[16,128]{1,0:T(8,128)S(1)}, f32[16,128]{1,0:T(8,128)S(1)}, u32[]{:S(2)}, u32[]{:S(2)}) collective-permute-start(f32[16,128]{1,0:T(8,128)S(1)} %add.43), channel_id=1, source_target_pairs={{0,1},{1,0},{2,3},{3,2},{4,5},{5,4},{6,7},{7,6},{8,9},{9,8},{10,11... | collective-permute-start | bytes 24584 | tf_op jit(solution)/shard_map/ppermute | solution.py:548
  (12 other events, 55.7 us)
where the time goes:
time: 182 us; the launch traced here: 183 us
  Pallas kernels  70.6 us (39%)
  waiting for transfers between devices  47.3 us (26%)
  starting transfers between devices  41 us (23%)
  local copies, waits for them, and re-layouts  20.7 us (11%)
  other arithmetic  2.57 us (1%)
    ppermute x12, starting transfers between devices, swap(): return lax.ppermute(value, axis, [(i, i ^ bits) for i in range(size)])  31.5 us
    ppermute x9, waiting for transfers between devices, gather(): moved.append(lax.ppermute(own, 'sec', pairs))  31.4 us
    pallas_call x3, Pallas kernels, chunk_call(): pl.pallas_call(functools.partial(chunk_kernel, first, last, held, chunk,...  30.9 us
    pallas_call x3, Pallas kernels, left_call(): pl.pallas_call(functools.partial(left_kernel, first, held, items, len(pay...  24.6 us
    unnamed x48, local copies, waits for them, and re-layouts  20 us
    ppermute x12, waiting for transfers between devices, swap(): return lax.ppermute(value, axis, [(i, i ^ bits) for i in range(size)])  16 us
    ppermute x9, starting transfers between devices, gather(): moved.append(lax.ppermute(own, 'sec', pairs))  9.46 us
    pallas_call x1, Pallas kernels, residual_call(): pl.pallas_call(functools.partial(residual_kernel, sectors // 2, slots), i...  6.6 us
  transfers between devices with their start and end apart: 21, of which 12 were waited for; matrix products, arithmetic and copies ran while one was open for 0% of the time, Pallas kernels for 26%

commit v1 on v0

--- a/solution.py
+++ b/solution.py
@@ -10,7 +10,7 @@
 TILE = 16
 WIDE = 2
 MIB = 1024 * 1024
-SPARE = 4 * MIB
+SPARE = 3 * MIB // 2
 HASTE = 256
 
 
@@ -439,7 +439,9 @@
         scratch_shapes=scratch,
         input_output_aliases=aliases,
         compiler_params=pltpu.CompilerParams(
-            vmem_limit_bytes=SPARE + 2 * every * wide * (wide + 2 * groups * width)
+            vmem_limit_bytes=(len(ahead) + len(late)) * SPARE // 4
+            + 2 * every * wide * (wide + 2 * groups * width)
+            + 4 * int(last) * states * width * width
         ),
         cost_estimate=pl.CostEstimate(
             flops=work // HASTE, bytes_accessed=psi.size // HASTE, transcendentals=0
@@ -551,7 +553,7 @@
         both = jnp.stack([near, received])
         return both, [swap(both, bits) for bits in range(2, devices, 2)]
 
-    chunks = [(0, terms // 2)] + [(at, 1) for at in range(terms // 2, terms)]
+    chunks = [(at, 1) for at in range(terms)]
     ordered = jnp.roll(places, -core * half)
     mine, theirs, *shares = pack_call(
         chunks, ordered, term_op, local_ops, left_env, right_env
@@ -601,25 +603,26 @@
     every = range(len(chunks))
     gather(None)
     token, live_psi, squares = go_left((0,), every, both_lefts, True)
-    token, = go_left((1,), every, token, waits=far_lefts)
     gather(token)
     token = choose(token)
+    token, = go_left((1,), every[1:], token, waits=far_lefts)
     total = None
     for at, chunk in enumerate(chunks):
         last = at == len(chunks) - 1
-        if at == len(chunks) - 2:
-            token, = go_left(far, [len(chunks) - 1], token)
         if len(rights) < len(chunks):
             token = choose(token)
         if len(shards) < len(chunks):
             gather(token)
         ahead = tuple(source for source in range(devices) if (at, source) in products)
         late = tuple(source for source in range(devices) if source not in ahead)
+        payloads = ([near_left] if 1 in late else []) + (far_lefts if late else [])
         total, token = chunk_call(
             at == 0, last, terms, chunk, ahead, late, scalars, slots, live_psi,
-            [products.pop((at, source)) for source in ahead], far_lefts if late else [],
+            [products.pop((at, source)) for source in ahead], payloads,
             rights[at], total, token,
         )
+        if at == len(chunks) - 3:
+            token, = go_left(far, [len(chunks) - 1], token)
 
     other = swap(total, 1)
     folds = jnp.concatenate([token, squares], axis=0)

time: 182 us -> 165 us (0.907)
  the two profiles are of different devices: /device:TPU:5 before, /device:TPU:0 now
where the time goes in v1:
time: 165 us; the launch traced here: 164 us
  Pallas kernels  83.9 us (51%)
  waiting for transfers between devices  39.3 us (24%)
  starting transfers between devices  27 us (16%)
  local copies, waits for them, and re-layouts  9.95 us (6%)
  other arithmetic  2.58 us (2%)
    pallas_call x4, Pallas kernels, chunk_call(): pl.pallas_call(functools.partial(chunk_kernel, first, last, held, chunk,...  42.4 us
    pallas_call x3, Pallas kernels, left_call(): pl.pallas_call(functools.partial(left_kernel, first, held, items, len(pay...  26.1 us
    ppermute x12, waiting for transfers between devices, gather(): moved.append(lax.ppermute(own, 'sec', pairs))  23.7 us
    ppermute x12, starting transfers between devices, gather(): moved.append(lax.ppermute(own, 'sec', pairs))  17.5 us
    ppermute x14, waiting for transfers between devices, swap(): return lax.ppermute(value, axis, [(i, i ^ bits) for i in range(size)])  15.6 us
    ppermute x14, starting transfers between devices, swap(): return lax.ppermute(value, axis, [(i, i ^ bits) for i in range(size)])  9.45 us
    unnamed x38, local copies, waits for them, and re-layouts  9.29 us
    pallas_call x1, Pallas kernels, residual_call(): pl.pallas_call(functools.partial(residual_kernel, sectors // 2, slots), i...  6.6 us
  transfers between devices with their start and end apart: 26, of which 12 were waited for; matrix products, arithmetic and copies ran while one was open for 1% of the time, Pallas kernels for 38%

profile of v1, /device:TPU:0, one launch (start us, length us, event | category | flops | bytes accessed | tf_op | source)
XLA Modules:
  0.0 163.8 jit_solution(10835993492844965828)
XLA Ops:
  2.5 3.7 %pack.1 = (bf16[2112,128]{1,0:T(8,128)(2,1)}, bf16[2112,128]{1,0:T(8,128)(2,1)}, bf16[8,1,128,128]{3,2,1,0:T(8,128)(2,1)}, bf16[8,1,128,128]{3,2,1,0:T(8,128)(2,...) custom-call(s32[8]{0:T(128)} %dynamic_slice.8.places, s32[4]{0:T(128)} %term_op.1, ...), custom_call_target="tpu_custom_call" | custom-call | bytes 2097152 | tf_op jit(solution)/shard_map/pack/pallas_call | solution.py:145
  6.8 4.7 %collective-permute-start.3 = (bf16[8,1,128,128]{3,2,1,0:T(8,128)(2,1)}, bf16[8,1,128,128]{3,2,1,0:T(8,128)(2,1)S(1)}, u32[]{:S(2)}, u32[]{:S(2)}) collective-permute-start(bf16[8,1,128,128]{3,2,1,0:T(8,128)(2,1)} %get-tuple-element.44.rest_1_), channel_id=1, source_target_pairs={{0,12},{4,0},{8,4},{12,8},{1,13},{5,1},{9,5},{13,9},{2,14},{6,2},{... | collective-permute-start | bytes 786440 | tf_op jit(solution)/shard_map/ppermute | solution.py:573
  13.6 1.6 collective-permute-start.5
  16.4 10.8 %left.3 = (bf16[8,1,8,256,128]{4,3,2,1,0:T(8,128)(2,1)S(1)}, bf16[8,1,8,256,128]{4,3,2,1,0:T(8,128)(2,1)S(1)}, bf16[8,1,8,256,128]{4,3,2,1,0:T(8,128)(2,1)S(1)},...) custom-call(s32[4]{0:T(128)S(1)} %pad_add_fusion.meta, ...), custom_call_target="tpu_custom_call" | custom-call | flops 25165824 | bytes 16384 | tf_op jit(solution)/shard_map/left/pallas_call | solution.py:255
  27.2 1.9 %copy-done.6 = bf16[8,1,8,256,128]{4,3,2,1,0:T(8,128)(2,1)} copy-done((bf16[8,1,8,256,128]{4,3,2,1,0:T(8,128)(2,1)}, bf16[8,1,8,256,128]{4,3,2,1,0:T(8,128)(2,1)S(1)}, u32[]{:S(2)}) %copy-start.6) | copy-done | bytes 4194328
  29.1 5.4 %collective-permute-done.2.rest_3_ = bf16[8,1,128,128]{3,2,1,0:T(8,128)(2,1)S(1)} collective-permute-done((bf16[8,1,128,128]{3,2,1,0:T(8,128)(2,1)}, bf16[8,1,128,128]{3,2,1,0:T(8,128)(2,1)S(1)}, u32[]{:S(2)}, u32[]{:S(2)}) %collective-permute-start.2) | collective-permute-done | bytes 262176 | tf_op jit(solution)/shard_map/ppermute | solution.py:573
  35.9 1.5 collective-permute-done.4
  37.5 1.6 collective-permute-start.6
  39.1 2.8 %collective-permute-start.8 = (bf16[8,1,128,128]{3,2,1,0:T(8,128)(2,1)S(1)}, bf16[8,1,128,128]{3,2,1,0:T(8,128)(2,1)S(1)}, u32[]{:S(2)}, u32[]{:S(2)}) collective-permute-start(bf16[8,1,128,128]{3,2,1,0:T(8,128)(2,1)S(1)} %copy-done.14), channel_id=1, source_target_pairs={{0,8},{4,12},{8,0},{12,4},{1,9},{5,13},{9,1},{13,5},{2,10},{6,14},... | collective-permute-start | bytes 786440 | tf_op jit(solution)/shard_map/ppermute | solution.py:573
  41.9 2.0 %collective-permute-start.7 = (bf16[8,1,128,128]{3,2,1,0:T(8,128)(2,1)S(1)}, bf16[8,1,128,128]{3,2,1,0:T(8,128)(2,1)S(1)}, u32[]{:S(2)}, u32[]{:S(2)}) collective-permute-start(bf16[8,1,128,128]{3,2,1,0:T(8,128)(2,1)S(1)} %copy-done.14), channel_id=1, source_target_pairs={{0,4},{4,8},{8,12},{12,0},{1,5},{5,9},{9,13},{13,1},{2,6},{6,10},{... | collective-permute-start | bytes 786440 | tf_op jit(solution)/shard_map/ppermute | solution.py:573
  43.9 8.4 %left.4 = (bf16[8,1,8,256,128]{4,3,2,1,0:T(8,128)(2,1)S(1)}, bf16[8,1,8,256,128]{4,3,2,1,0:T(8,128)(2,1)S(1)}, bf16[8,1,8,256,128]{4,3,2,1,0:T(8,128)(2,1)S(1)}, f32[8,128]{1,0:T(8,128)S(1)}) custom-call(s32[4]{0:T(128)S(1)} %pad_add_fusion.meta, s32[8]{0:T(128)S(1)} %select_reduce_fusion.places, s32[32]{0:T(128)S(1)} %copy-done.16, ...), custom_call_target="tpu_custom_call" | custom-call | flops 9437184 | bytes 8192 | tf_op jit(solution)/shard_map/left/pallas_call | solution.py:255
  52.3 1.9 %copy-done.2 = bf16[8,1,8,256,128]{4,3,2,1,0:T(8,128)(2,1)} copy-done((bf16[8,1,8,256,128]{4,3,2,1,0:T(8,128)(2,1)}, bf16[8,1,8,256,128]{4,3,2,1,0:T(8,128)(2,1)S(1)}, u32[]{:S(2)}) %copy-start.2) | copy-done | bytes 4194328
  54.2 2.1 %copy-done.8 = bf16[8,1,8,256,128]{4,3,2,1,0:T(8,128)(2,1)} copy-done((bf16[8,1,8,256,128]{4,3,2,1,0:T(8,128)(2,1)}, bf16[8,1,8,256,128]{4,3,2,1,0:T(8,128)(2,1)S(1)}, u32[]{:S(2)}) %copy-start.8) | copy-done | bytes 4194328
  56.3 8.7 %collective-permute-done.8.rest_4_ = bf16[8,1,128,128]{3,2,1,0:T(8,128)(2,1)S(1)} collective-permute-done((bf16[8,1,128,128]{3,2,1,0:T(8,128)(2,1)S(1)}, bf16[8,1,128,128]{3,2,1,0:T(8,128)(2,1)S(1)}, u32[]{:S(2)}, u32[]{:S(2)}) %collective-permute-start.8) | collective-permute-done | bytes 262176 | tf_op jit(solution)/shard_map/ppermute | solution.py:573
  66.4 1.5 collective-permute-done.10
  68.8 2.0 %collective-permute-start.12 = (bf16[8,1,128,128]{3,2,1,0:T(8,128)(2,1)S(1)}, bf16[8,1,128,128]{3,2,1,0:T(8,128)(2,1)S(1)}, u32[]{:S(2)}, u32[]{:S(2)}) collective-permute-start(bf16[8,1,128,128]{3,2,1,0:T(8,128)(2,1)S(1)} %copy-done.13), channel_id=1, source_target_pairs={{0,4},{4,8},{8,12},{12,0},{1,5},{5,9},{9,13},{13,1},{2,6},{6,10},{... | collective-permute-start | bytes 786440 | tf_op jit(solution)/shard_map/ppermute | solution.py:573
  70.8 2.2 %copy-done.5 = bf16[8,1,8,256,128]{4,3,2,1,0:T(8,128)(2,1)S(1)} copy-done((bf16[8,1,8,256,128]{4,3,2,1,0:T(8,128)(2,1)S(1)}, bf16[8,1,8,256,128]{4,3,2,1,0:T(8,128)(2,1)}, u32[]{:S(2)}) %copy-start.5) | copy-done | bytes 4194328
  73.0 13.0 %chunk.4 = (f32[8,16,128,128]{3,2,1,0:T(8,128)S(1)}, f32[8,128]{1,0:T(8,128)S(1)}) custom-call(s32[4]{0:T(128)S(1)} %pad_add_fusion.meta, s32[8]{0:T(128)S(1)} %select_reduce_fusion.places, s32[32]{0:T(128)S(1)} %copy-done.16, s32[8,2]{1,0:T(8,128)S(1)} %copy.51.partners, s32[8]{0:T(128)S(1)} %copy-done.15, ...), custom_call_target="tpu_custom_call" | custom-call | flops 13631488 | bytes 8192 | tf_op jit(solution)/shard_map/chunk/pallas_call | solution.py:426
  86.0 5.9 %collective-permute-done.13.rest_4_ = bf16[8,1,128,128]{3,2,1,0:T(8,128)(2,1)S(1)} collective-permute-done((bf16[8,1,128,128]{3,2,1,0:T(8,128)(2,1)S(1)}, bf16[8,1,128,128]{3,2,1,0:T(8,128)(2,1)S(1)}, u32[]{:S(2)}, u32[]{:S(2)}) %collective-permute-start.13) | collective-permute-done | bytes 262176 | tf_op jit(solution)/shard_map/ppermute | solution.py:573
  94.9 1.6 collective-permute-start.16
  96.4 2.8 %collective-permute-start.18 = (bf16[8,1,128,128]{3,2,1,0:T(8,128)(2,1)S(1)}, bf16[8,1,128,128]{3,2,1,0:T(8,128)(2,1)S(1)}, u32[]{:S(2)}, u32[]{:S(2)}) collective-permute-start(bf16[8,1,128,128]{3,2,1,0:T(8,128)(2,1)S(1)} %copy-done.12), channel_id=1, source_target_pairs={{0,8},{4,12},{8,0},{12,4},{1,9},{5,13},{9,1},{13,5},{2,10},{6,14},... | collective-permute-start | bytes 786440 | tf_op jit(solution)/shard_map/ppermute | solution.py:573
  99.2 2.0 %collective-permute-start.17 = (bf16[8,1,128,128]{3,2,1,0:T(8,128)(2,1)S(1)}, bf16[8,1,128,128]{3,2,1,0:T(8,128)(2,1)S(1)}, u32[]{:S(2)}, u32[]{:S(2)}) collective-permute-start(bf16[8,1,128,128]{3,2,1,0:T(8,128)(2,1)S(1)} %copy-done.12), channel_id=1, source_target_pairs={{0,4},{4,8},{8,12},{12,0},{1,5},{5,9},{9,13},{13,1},{2,6},{6,10},{... | collective-permute-start | bytes 786440 | tf_op jit(solution)/shard_map/ppermute | solution.py:573
  101.3 10.7 %chunk.5 = (f32[8,16,128,128]{3,2,1,0:T(8,128)S(1)}, f32[8,128]{1,0:T(8,128)S(1)}) custom-call(s32[4]{0:T(128)S(1)} %pad_add_fusion.meta, s32[8]{0:T(128)S(1)} %select_reduce_fusion.places, s32[32]{0:T(128)S(1)} %copy-done.16, s32[8,2]{1,0:T(8,128)S(1)} %copy.51.partners, s32[8]{0:T(128)S(1)} %copy-done.15, ...), custom_call_target="tpu_custom_call", output_to_operand_aliasing={{0}: (13, {})} | custom-call | flops 10485760 | bytes 8192 | tf_op jit(solution)/shard_map/chunk/pallas_call | solution.py:426
  111.9 6.9 %left.5 = (bf16[8,1,8,256,128]{4,3,2,1,0:T(8,128)(2,1)S(1)}, bf16[8,1,8,256,128]{4,3,2,1,0:T(8,128)(2,1)S(1)}, f32[8,128]{1,0:T(8,128)S(1)}) custom-call(s32[4]{0:T(128)S(1)} %pad_add_fusion.meta, s32[8]{0:T(128)S(1)} %select_reduce_fusion.places, s32[32]{0:T(128)S(1)} %copy-done.16, s32[8,2]{1,0:T(8,128)S(1)} %copy.51.partners, s32[8]{0:T(128)S(1)} %copy-done.15, ...), custom_call_target="tpu_custom_call" | custom-call | flops 6291456 | bytes 8192 | tf_op jit(solution)/shard_map/left/pallas_call | solution.py:255
  118.8 3.6 %collective-permute-done.18.rest_4_ = bf16[8,1,128,128]{3,2,1,0:T(8,128)(2,1)S(1)} collective-permute-done((bf16[8,1,128,128]{3,2,1,0:T(8,128)(2,1)S(1)}, bf16[8,1,128,128]{3,2,1,0:T(8,128)(2,1)S(1)}, u32[]{:S(2)}, u32[]{:S(2)}) %collective-permute-start.18) | collective-permute-done | bytes 262176 | tf_op jit(solution)/shard_map/ppermute | solution.py:573
  126.0 10.6 %chunk.6 = (f32[8,16,128,128]{3,2,1,0:T(8,128)S(1)}, f32[8,128]{1,0:T(8,128)S(1)}) custom-call(s32[4]{0:T(128)S(1)} %pad_add_fusion.meta, s32[8]{0:T(128)S(1)} %select_reduce_fusion.places, s32[32]{0:T(128)S(1)} %copy-done.16, s32[8,2]{1,0:T(8,128)S(1)} %copy.51.partners, s32[8]{0:T(128)S(1)} %copy-done.15, ...), custom_call_target="tpu_custom_call", output_to_operand_aliasing={{0}: (13, {})} | custom-call | flops 10485760 | bytes 8192 | tf_op jit(solution)/shard_map/chunk/pallas_call | solution.py:426
  136.6 2.8 %collective-permute-done.21.rest_6_ = bf16[2,8,1,128,128]{4,3,2,1,0:T(8,128)(2,1)S(1)} collective-permute-done((bf16[2,8,1,128,128]{4,3,2,1,0:T(8,128)(2,1)S(1)}, bf16[2,8,1,128,128]{4,3,2,1,0:T(8,128)(2,1)S(1)}, u32[]{:S(2)}, u32[]{:S(2)}) %collective-permute-start.21) | collective-permute-done | bytes 524320 | tf_op jit(solution)/shard_map/ppermute | solution.py:550
  139.4 8.1 %chunk.7 = (bf16[8,16,128,128]{3,2,1,0:T(8,128)(2,1)S(1)}, f32[8,128]{1,0:T(8,128)S(1)}) custom-call(s32[4]{0:T(128)S(1)} %pad_add_fusion.meta, s32[8]{0:T(128)S(1)} %select_reduce_fusion.places, s32[32]{0:T(128)S(1)} %copy-done.16, s32[8,2]{1,0:T(8,128)S(1)} %copy.51.partners, s32[8]{0:T(128)S(1)} %copy-done.15, f32[8,128]{1,0:T(8,128)S(1)} %get-tuple-element.71.after_ref, ...), custom_call_target="tpu_custom_call" | custom-call | flops 4194304 | bytes 8192 | tf_op jit(solution)/shard_map/chunk/pallas_call | solution.py:426
  148.5 2.9 %collective-permute-done.22 = f32[16,128]{1,0:T(8,128)S(1)} collective-permute-done((f32[16,128]{1,0:T(8,128)S(1)}, f32[16,128]{1,0:T(8,128)S(1)}, u32[]{:S(2)}, u32[]{:S(2)}) %collective-permute-start.22) | collective-permute-done | bytes 8224 | tf_op jit(solution)/shard_map/ppermute | solution.py:550
  151.4 1.9 %collective-permute-start.23 = (f32[16,128]{1,0:T(8,128)S(1)}, f32[16,128]{1,0:T(8,128)S(1)}, u32[]{:S(2)}, u32[]{:S(2)}) collective-permute-start(f32[16,128]{1,0:T(8,128)S(1)} %add.42), channel_id=1, source_target_pairs={{0,8},{4,12},{8,0},{12,4},{1,9},{5,13},{9,1},{13,5},{2,10},{6,14},... | collective-permute-start | bytes 24584 | tf_op jit(solution)/shard_map/ppermute | solution.py:550
  153.2 2.7 %collective-permute-done.23 = f32[16,128]{1,0:T(8,128)S(1)} collective-permute-done((f32[16,128]{1,0:T(8,128)S(1)}, f32[16,128]{1,0:T(8,128)S(1)}, u32[]{:S(2)}, u32[]{:S(2)}) %collective-permute-start.23) | collective-permute-done | bytes 8224 | tf_op jit(solution)/shard_map/ppermute | solution.py:550
  157.1 6.6 %residual.1 = (bf16[8,2,16,128,128]{4,3,2,1,0:T(8,128)(2,1)}, f32[1]{0:T(128)}) custom-call(s32[4]{0:T(128)S(1)} %pad_add_fusion.meta, s32[8]{0:T(128)S(1)} %select_reduce_fusion.places, s32[32]{0:T(128)S(1)} %copy-done.16, s32[8,2]{1,0:T(8,128)S(1)} %copy.51.partners, s32[8]{0:T(128)S(1)} %copy-done.15, f32[16,128]{1,0:T(8,128)S(1)} %add.44.folds_ref, ...), custom_call_target="tpu_custom_call" | custom-call | flops 12582912 | bytes 25165824 | tf_op jit(solution)/shard_map/residual/pallas_call | solution.py:504
  (87 shorter events, 17.9 us)
Async XLA Ops:
  6.2 6.2 %collective-permute-start = (bf16[2112,128]{1,0:T(8,128)(2,1)}, bf16[2112,128]{1,0:T(8,128)(2,1)S(1)}, u32[]{:S(2)}, u32[]{:S(2)}) collective-permute-start(bf16[2112,128]{1,0:T(8,128)(2,1)} %get-tuple-element.42), channel_id=1, source_target_pairs={{0,1},{1,0},{2,3},{3,2},{4,5},{5,4},{6,7},{7,6},{8,9},{9,8},{10,11... | collective-permute-start | bytes 1622024 | tf_op jit(solution)/shard_map/ppermute | solution.py:550
  6.8 22.4 %collective-permute-start.3 = (bf16[8,1,128,128]{3,2,1,0:T(8,128)(2,1)}, bf16[8,1,128,128]{3,2,1,0:T(8,128)(2,1)S(1)}, u32[]{:S(2)}, u32[]{:S(2)}) collective-permute-start(bf16[8,1,128,128]{3,2,1,0:T(8,128)(2,1)} %get-tuple-element.44.rest_1_), channel_id=1, source_target_pairs={{0,12},{4,0},{8,4},{12,8},{1,13},{5,1},{9,5},{13,9},{2,14},{6,2},{... | collective-permute-start | bytes 786440 | tf_op jit(solution)/shard_map/ppermute | solution.py:573
  11.4 23.1 %collective-permute-start.2 = (bf16[8,1,128,128]{3,2,1,0:T(8,128)(2,1)}, bf16[8,1,128,128]{3,2,1,0:T(8,128)(2,1)S(1)}, u32[]{:S(2)}, u32[]{:S(2)}) collective-permute-start(bf16[8,1,128,128]{3,2,1,0:T(8,128)(2,1)} %get-tuple-element.44.rest_1_), channel_id=1, source_target_pairs={{0,8},{4,12},{8,0},{12,4},{1,9},{5,13},{9,1},{13,5},{2,10},{6,14},... | collective-permute-start | bytes 786440 | tf_op jit(solution)/shard_map/ppermute | solution.py:573
  11.4 23.1 %collective-permute-start.1 = (bf16[8,1,128,128]{3,2,1,0:T(8,128)(2,1)}, bf16[8,1,128,128]{3,2,1,0:T(8,128)(2,1)S(1)}, u32[]{:S(2)}, u32[]{:S(2)}) collective-permute-start(bf16[8,1,128,128]{3,2,1,0:T(8,128)(2,1)} %get-tuple-element.44.rest_1_), channel_id=1, source_target_pairs={{0,4},{4,8},{8,12},{12,0},{1,5},{5,9},{9,13},{13,1},{2,6},{6,10},{... | collective-permute-start | bytes 786440 | tf_op jit(solution)/shard_map/ppermute | solution.py:573
  13.6 30.3 %collective-permute-start.5 = (bf16[2,2112,128]{2,1,0:T(8,128)(2,1)S(1)}, bf16[2,2112,128]{2,1,0:T(8,128)(2,1)S(1)}, u32[]{:S(2)}, u32[]{:S(2)}) collective-permute-start(bf16[2,2112,128]{2,1,0:T(8,128)(2,1)S(1)} %pad_maximum_fusion.rest_0_), channel_id=1, source_target_pairs={{0,2},{1,3},{2,0},{3,1},{4,6},{5,7},{6,4},{7,5},{8,10},{9,11},{10,... | collective-permute-start | bytes 3244040 | tf_op jit(solution)/shard_map/ppermute | solution.py:550
  29.1 23.2 %copy-start = (bf16[8,1,8,256,128]{4,3,2,1,0:T(8,128)(2,1)}, bf16[8,1,8,256,128]{4,3,2,1,0:T(8,128)(2,1)S(1)}, u32[]{:S(2)}) copy-start(bf16[8,1,8,256,128]{4,3,2,1,0:T(8,128)(2,1)S(1)} %get-tuple-element.59.rest_0_) | copy-start | bytes 12582916
  29.1 23.2 %copy-start.4 = (bf16[8,1,8,256,128]{4,3,2,1,0:T(8,128)(2,1)}, bf16[8,1,8,256,128]{4,3,2,1,0:T(8,128)(2,1)S(1)}, u32[]{:S(2)}) copy-start(bf16[8,1,8,256,128]{4,3,2,1,0:T(8,128)(2,1)S(1)} %get-tuple-element.53.rest_0_) | copy-start | bytes 12582916
  35.8 1.6 collective-permute-start.4
  37.5 27.5 %collective-permute-start.6 = (bf16[2,8,1,128,128]{4,3,2,1,0:T(8,128)(2,1)S(1)}, bf16[2,8,1,128,128]{4,3,2,1,0:T(8,128)(2,1)S(1)}, u32[]{:S(2)}, u32[]{:S(2)}) collective-permute-start(bf16[2,8,1,128,128]{4,3,2,1,0:T(8,128)(2,1)S(1)} %pad_maximum_fusion.1.rest_0_), channel_id=1, source_target_pairs={{0,2},{1,3},{2,0},{3,1},{4,6},{5,7},{6,4},{7,5},{8,10},{9,11},{10,... | collective-permute-start | bytes 1572872 | tf_op jit(solution)/shard_map/ppermute | solution.py:550
  39.1 17.2 %collective-permute-start.9 = (bf16[8,1,128,128]{3,2,1,0:T(8,128)(2,1)S(1)}, bf16[8,1,128,128]{3,2,1,0:T(8,128)(2,1)S(1)}, u32[]{:S(2)}, u32[]{:S(2)}) collective-permute-start(bf16[8,1,128,128]{3,2,1,0:T(8,128)(2,1)S(1)} %copy-done.14), channel_id=1, source_target_pairs={{0,12},{4,0},{8,4},{12,8},{1,13},{5,1},{9,5},{13,9},{2,14},{6,2},{... | collective-permute-start | bytes 786440 | tf_op jit(solution)/shard_map/ppermute | solution.py:573
  39.1 26.0 %collective-permute-start.8 = (bf16[8,1,128,128]{3,2,1,0:T(8,128)(2,1)S(1)}, bf16[8,1,128,128]{3,2,1,0:T(8,128)(2,1)S(1)}, u32[]{:S(2)}, u32[]{:S(2)}) collective-permute-start(bf16[8,1,128,128]{3,2,1,0:T(8,128)(2,1)S(1)} %copy-done.14), channel_id=1, source_target_pairs={{0,8},{4,12},{8,0},{12,4},{1,9},{5,13},{9,1},{13,5},{2,10},{6,14},... | collective-permute-start | bytes 786440 | tf_op jit(solution)/shard_map/ppermute | solution.py:573
  41.9 23.2 %collective-permute-start.7 = (bf16[8,1,128,128]{3,2,1,0:T(8,128)(2,1)S(1)}, bf16[8,1,128,128]{3,2,1,0:T(8,128)(2,1)S(1)}, u32[]{:S(2)}, u32[]{:S(2)}) collective-permute-start(bf16[8,1,128,128]{3,2,1,0:T(8,128)(2,1)S(1)} %copy-done.14), channel_id=1, source_target_pairs={{0,4},{4,8},{8,12},{12,0},{1,5},{5,9},{9,13},{13,1},{2,6},{6,10},{... | collective-permute-start | bytes 786440 | tf_op jit(solution)/shard_map/ppermute | solution.py:573
  43.9 24.7 %copy-start.13 = (bf16[8,1,128,128]{3,2,1,0:T(8,128)(2,1)S(1)}, bf16[8,1,128,128]{3,2,1,0:T(8,128)(2,1)}, u32[]{:S(2)}) copy-start(bf16[8,1,128,128]{3,2,1,0:T(8,128)(2,1)} %get-tuple-element.56.rest_2_) | copy-start | bytes 786436
  66.3 1.6 collective-permute-start.10
  68.0 24.0 %collective-permute-start.11 = (bf16[2,8,1,128,128]{4,3,2,1,0:T(8,128)(2,1)S(1)}, bf16[2,8,1,128,128]{4,3,2,1,0:T(8,128)(2,1)S(1)}, u32[]{:S(2)}, u32[]{:S(2)}) collective-permute-start(bf16[2,8,1,128,128]{4,3,2,1,0:T(8,128)(2,1)S(1)} %pad_maximum_fusion.2.after_ref), channel_id=1, source_target_pairs={{0,2},{1,3},{2,0},{3,1},{4,6},{5,7},{6,4},{7,5},{8,10},{9,11},{10,... | collective-permute-start | bytes 1572872 | tf_op jit(solution)/shard_map/ppermute | solution.py:550
  68.6 17.4 %collective-permute-start.14 = (bf16[8,1,128,128]{3,2,1,0:T(8,128)(2,1)S(1)}, bf16[8,1,128,128]{3,2,1,0:T(8,128)(2,1)S(1)}, u32[]{:S(2)}, u32[]{:S(2)}) collective-permute-start(bf16[8,1,128,128]{3,2,1,0:T(8,128)(2,1)S(1)} %copy-done.13), channel_id=1, source_target_pairs={{0,12},{4,0},{8,4},{12,8},{1,13},{5,1},{9,5},{13,9},{2,14},{6,2},{... | collective-permute-start | bytes 786440 | tf_op jit(solution)/shard_map/ppermute | solution.py:573
  68.6 23.3 %collective-permute-start.13 = (bf16[8,1,128,128]{3,2,1,0:T(8,128)(2,1)S(1)}, bf16[8,1,128,128]{3,2,1,0:T(8,128)(2,1)S(1)}, u32[]{:S(2)}, u32[]{:S(2)}) collective-permute-start(bf16[8,1,128,128]{3,2,1,0:T(8,128)(2,1)S(1)} %copy-done.13), channel_id=1, source_target_pairs={{0,8},{4,12},{8,0},{12,4},{1,9},{5,13},{9,1},{13,5},{2,10},{6,14},... | collective-permute-start | bytes 786440 | tf_op jit(solution)/shard_map/ppermute | solution.py:573
  68.8 23.2 %collective-permute-start.12 = (bf16[8,1,128,128]{3,2,1,0:T(8,128)(2,1)S(1)}, bf16[8,1,128,128]{3,2,1,0:T(8,128)(2,1)S(1)}, u32[]{:S(2)}, u32[]{:S(2)}) collective-permute-start(bf16[8,1,128,128]{3,2,1,0:T(8,128)(2,1)S(1)} %copy-done.13), channel_id=1, source_target_pairs={{0,4},{4,8},{8,12},{12,0},{1,5},{5,9},{9,13},{13,1},{2,6},{6,10},{... | collective-permute-start | bytes 786440 | tf_op jit(solution)/shard_map/ppermute | solution.py:573
  73.0 23.5 %copy-start.12 = (bf16[8,1,128,128]{3,2,1,0:T(8,128)(2,1)S(1)}, bf16[8,1,128,128]{3,2,1,0:T(8,128)(2,1)}, u32[]{:S(2)}) copy-start(bf16[8,1,128,128]{3,2,1,0:T(8,128)(2,1)} %get-tuple-element.65.rest_2_) | copy-start | bytes 786436
  73.0 28.3 %copy-start.1 = (bf16[8,1,8,256,128]{4,3,2,1,0:T(8,128)(2,1)S(1)}, bf16[8,1,8,256,128]{4,3,2,1,0:T(8,128)(2,1)}, u32[]{:S(2)}) copy-start(bf16[8,1,8,256,128]{4,3,2,1,0:T(8,128)(2,1)} %copy-done) | copy-start | bytes 12582916
  73.0 28.3 %copy-start.3 = (bf16[8,1,8,256,128]{4,3,2,1,0:T(8,128)(2,1)S(1)}, bf16[8,1,8,256,128]{4,3,2,1,0:T(8,128)(2,1)}, u32[]{:S(2)}) copy-start(bf16[8,1,8,256,128]{4,3,2,1,0:T(8,128)(2,1)} %copy-done.2) | copy-start | bytes 12582916
  93.2 1.6 collective-permute-start.15
  94.9 27.5 %collective-permute-start.16 = (bf16[2,8,1,128,128]{4,3,2,1,0:T(8,128)(2,1)S(1)}, bf16[2,8,1,128,128]{4,3,2,1,0:T(8,128)(2,1)S(1)}, u32[]{:S(2)}, u32[]{:S(2)}) collective-permute-start(bf16[2,8,1,128,128]{4,3,2,1,0:T(8,128)(2,1)S(1)} %pad_maximum_fusion.3.after_ref), channel_id=1, source_target_pairs={{0,2},{1,3},{2,0},{3,1},{4,6},{5,7},{6,4},{7,5},{8,10},{9,11},{10,... | collective-permute-start | bytes 1572872 | tf_op jit(solution)/shard_map/ppermute | solution.py:550
  96.4 22.4 %collective-permute-start.19 = (bf16[8,1,128,128]{3,2,1,0:T(8,128)(2,1)S(1)}, bf16[8,1,128,128]{3,2,1,0:T(8,128)(2,1)S(1)}, u32[]{:S(2)}, u32[]{:S(2)}) collective-permute-start(bf16[8,1,128,128]{3,2,1,0:T(8,128)(2,1)S(1)} %copy-done.12), channel_id=1, source_target_pairs={{0,12},{4,0},{8,4},{12,8},{1,13},{5,1},{9,5},{13,9},{2,14},{6,2},{... | collective-permute-start | bytes 786440 | tf_op jit(solution)/shard_map/ppermute | solution.py:573
  96.4 26.0 %collective-permute-start.18 = (bf16[8,1,128,128]{3,2,1,0:T(8,128)(2,1)S(1)}, bf16[8,1,128,128]{3,2,1,0:T(8,128)(2,1)S(1)}, u32[]{:S(2)}, u32[]{:S(2)}) collective-permute-start(bf16[8,1,128,128]{3,2,1,0:T(8,128)(2,1)S(1)} %copy-done.12), channel_id=1, source_target_pairs={{0,8},{4,12},{8,0},{12,4},{1,9},{5,13},{9,1},{13,5},{2,10},{6,14},... | collective-permute-start | bytes 786440 | tf_op jit(solution)/shard_map/ppermute | solution.py:573
  99.2 23.2 %collective-permute-start.17 = (bf16[8,1,128,128]{3,2,1,0:T(8,128)(2,1)S(1)}, bf16[8,1,128,128]{3,2,1,0:T(8,128)(2,1)S(1)}, u32[]{:S(2)}, u32[]{:S(2)}) collective-permute-start(bf16[8,1,128,128]{3,2,1,0:T(8,128)(2,1)S(1)} %copy-done.12), channel_id=1, source_target_pairs={{0,4},{4,8},{8,12},{12,0},{1,5},{5,9},{9,13},{13,1},{2,6},{6,10},{... | collective-permute-start | bytes 786440 | tf_op jit(solution)/shard_map/ppermute | solution.py:573
  123.7 1.6 collective-permute-start.20
  125.4 14.0 %collective-permute-start.21 = (bf16[2,8,1,128,128]{4,3,2,1,0:T(8,128)(2,1)S(1)}, bf16[2,8,1,128,128]{4,3,2,1,0:T(8,128)(2,1)S(1)}, u32[]{:S(2)}, u32[]{:S(2)}) collective-permute-start(bf16[2,8,1,128,128]{4,3,2,1,0:T(8,128)(2,1)S(1)} %pad_maximum_fusion.4.after_ref), channel_id=1, source_target_pairs={{0,2},{1,3},{2,0},{3,1},{4,6},{5,7},{6,4},{7,5},{8,10},{9,11},{10,... | collective-permute-start | bytes 1572872 | tf_op jit(solution)/shard_map/ppermute | solution.py:550
  147.5 9.6 %collective-permute-start.25 = (bf16[8,16,128,128]{3,2,1,0:T(8,128)(2,1)S(1)}, bf16[8,16,128,128]{3,2,1,0:T(8,128)(2,1)S(1)}, u32[]{:S(2)}, u32[]{:S(2)}) collective-permute-start(bf16[8,16,128,128]{3,2,1,0:T(8,128)(2,1)S(1)} %get-tuple-element.79.own_ref), channel_id=1, source_target_pairs={{0,1},{1,0},{2,3},{3,2},{4,5},{5,4},{6,7},{7,6},{8,9},{9,8},{10,11... | collective-permute-start | bytes 12582920 | tf_op jit(solution)/shard_map/ppermute | solution.py:550
  147.6 3.7 %collective-permute-start.22 = (f32[16,128]{1,0:T(8,128)S(1)}, f32[16,128]{1,0:T(8,128)S(1)}, u32[]{:S(2)}, u32[]{:S(2)}) collective-permute-start(f32[16,128]{1,0:T(8,128)S(1)} %constant_dynamic-update-slice_fusion), channel_id=1, source_target_pairs={{0,4},{4,0},{8,12},{12,8},{1,5},{5,1},{9,13},{13,9},{2,6},{6,2},{1... | collective-permute-start | bytes 24584 | tf_op jit(solution)/shard_map/ppermute | solution.py:550
  151.4 4.5 %collective-permute-start.23 = (f32[16,128]{1,0:T(8,128)S(1)}, f32[16,128]{1,0:T(8,128)S(1)}, u32[]{:S(2)}, u32[]{:S(2)}) collective-permute-start(f32[16,128]{1,0:T(8,128)S(1)} %add.42), channel_id=1, source_target_pairs={{0,8},{4,12},{8,0},{12,4},{1,9},{5,13},{9,1},{13,5},{2,10},{6,14},... | collective-permute-start | bytes 24584 | tf_op jit(solution)/shard_map/ppermute | solution.py:550
  155.9 1.2 collective-permute-start.24
  (12 other events, 120.8 us)

commit v2 on v1

--- a/solution.py
+++ b/solution.py
@@ -35,10 +35,9 @@
 
 
 def by_live_rows(own_rows, groups, work):
-    always = groups // 2
-    work(0, always)
-    for group in range(always, groups, WIDE):
-        pl.when(own_rows > group * TILE)(functools.partial(work, group, group + WIDE))
+    few = 3 * groups // 4
+    pl.when(own_rows <= few * TILE)(functools.partial(work, few))
+    pl.when(own_rows > few * TILE)(functools.partial(work, groups))
 
 
 def spread_operators(ops_ref, chosen, spread_ops, at, states):
@@ -61,17 +60,18 @@
         at += 1
 
 
-def multiply_left(lefts, live_psi, after_left):
-    terms, groups = after_left.shape[:2]
+def multiply_left(groups, lefts, live_psi, after_left):
+    rows = groups * TILE
     states, width = live_psi.shape[0], live_psi.shape[-1]
+    stacked = jnp.concatenate(lefts, axis=0)
     for pair in range(states // WIDE):
         columns = jnp.concatenate([live_psi[pair * WIDE + at] for at in range(WIDE)], axis=1)
-        done = jnp.dot(lefts, columns, preferred_element_type=jnp.float32).astype(jnp.bfloat16)
-        for term in range(terms):
+        done = jnp.dot(stacked, columns, preferred_element_type=jnp.float32).astype(jnp.bfloat16)
+        for term in range(len(lefts)):
             for at in range(WIDE):
                 state = pair * WIDE + at
-                after_left[term, :, state * TILE : (state + 1) * TILE, :] = done[
-                    term * width : (term + 1) * width, at * width : (at + 1) * width
+                after_left[term, :groups, state * TILE : (state + 1) * TILE, :] = done[
+                    term * rows : (term + 1) * rows, at * width : (at + 1) * width
                 ].reshape(groups, TILE, width)
 
 
@@ -163,8 +163,9 @@
     return views
 
 
-def term_rows(place, held, start, terms, width):
-    return pl.ds(pl.multiple_of((place * held + start) * width, width), terms * width)
+def term_rows(view, place, held, term, rows):
+    width = view.shape[-1]
+    return view[pl.ds(pl.multiple_of((place * held + term) * width, width), rows), :]
 
 
 def left_kernel(first, held, items, count, afters, half, slots, meta, places, sector_rows,
@@ -207,21 +208,22 @@
             live_psi[block] = kept
             wide_psi = kept.astype(jnp.float32)
             square_ref[...] += folded(wide_psi * wide_psi)
-        lefts = [
-            views[source][term_rows(place, held, start, terms, width), :]
-            for source, start, terms in items
-        ]
-        multiply_left(jnp.concatenate(lefts, axis=0), live_psi.at[block], after_left)
         targets = [
             (outs[at], (block, term))
             for at, (source, start, terms) in enumerate(items)
             for term in range(terms)
         ]
-        by_live_rows(
-            own_rows,
-            width // TILE,
-            lambda low, high: apply_operators(low, high, spread_ops, after_left, targets),
-        )
+
+        def multiply(groups):
+            lefts = [
+                term_rows(views[source], place, held, start + term, groups * TILE)
+                for source, start, terms in items
+                for term in range(terms)
+            ]
+            multiply_left(groups, lefts, live_psi.at[block], after_left)
+            apply_operators(0, groups, spread_ops, after_left, targets)
+
+        by_live_rows(own_rows, width // TILE, multiply)
 
     each_live_block(half, slots, scalars, work)
 
@@ -276,6 +278,23 @@
         ),
         name="left",
     )(*scalars, *afters, psi, *payloads)
+
+
+def stack_kernel(near_ref, received_ref, both_ref):
+    both_ref[0] = near_ref[...]
+    both_ref[1] = received_ref[...]
+
+
+def stack_call(near, received):
+    return pl.pallas_call(
+        stack_kernel,
+        in_specs=resident(2),
+        out_specs=resident(1)[0],
+        out_shape=jax.ShapeDtypeStruct((2,) + near.shape, near.dtype),
+        compiler_params=pltpu.CompilerParams(vmem_limit_bytes=SPARE),
+        cost_estimate=pl.CostEstimate(flops=0, bytes_accessed=8 * near.size, transcendentals=0),
+        name="stack",
+    )(near, received)
 
 
 def choose_kernel(devices, afters, sectors, half, slots, meta, places, partners, *rest):
@@ -338,11 +357,6 @@
 
     def work(block, place, sector, own_rows, partner_rows):
         total = rest[0] if last else sum_out.at[block]
-        if late:
-            lefts = [
-                views[source][term_rows(place, held, start, terms, width), :] for source in late
-            ]
-            multiply_left(jnp.concatenate(lefts, axis=0), psi_ref.at[block], after_left)
         columns = [
             jnp.concatenate(
                 [rights[pair + at][block, term] for at in range(2) for term in range(terms)],
@@ -356,11 +370,18 @@
                 return early_refs[ahead.index(device)][block, term, group]
             return after_ops[late.index(device) * terms + term, group]
 
-        def multiply(low, high):
+        def multiply(live_groups):
             if late:
-                targets = [(after_ops, (term,)) for term in range(len(late) * terms)]
-                apply_operators(low, high, spread_ops, after_left, targets)
-            for group in range(low, high, WIDE):
+                lefts = [
+                    term_rows(views[source], place, held, start + term, live_groups * TILE)
+                    for source in late
+                    for term in range(terms)
+                ]
+                multiply_left(live_groups, lefts, psi_ref.at[block], after_left)
+            targets = [(after_ops, (term,)) for term in range(len(late) * terms)]
+            for group in range(0, live_groups, WIDE):
+                if late:
+                    apply_operators(group, group + WIDE, spread_ops, after_left, targets)
                 parts = []
                 for pair in range(0, devices, 2):
                     rows = jnp.concatenate(
@@ -550,7 +571,7 @@
         return lax.ppermute(value, axis, [(i, i ^ bits) for i in range(size)])
 
     def to_far_chips(near, received):
-        both = jnp.stack([near, received])
+        both = stack_call(near, received)
         return both, [swap(both, bits) for bits in range(2, devices, 2)]
 
     chunks = [(at, 1) for at in range(terms)]

time: 165 us -> 167 us (1.012)
  Pallas kernels: 83.9 us -> 88 us
  waiting for transfers between devices: 39.3 us -> 41.2 us
    pallas_call x4, Pallas kernels: 42.4 us -> 45.1 us  [chunk_call(): pl.pallas_call(functools.partial(chunk_kernel, first, last, held, chunk,...]
    unnamed x38 -> x36, local copies, waits for them, and re-layouts: 9.29 us -> 8.46 us
  transfers between devices with their start and end apart: 26 -> 26, of which waited for: 12 -> 13; matrix products, arithmetic and copies ran while one was open for 1% -> 0% of each run, Pallas kernels for 38% -> 39%
where the time goes in v2:
time: 167 us
  Pallas kernels  88 us (53%)
  waiting for transfers between devices  41.2 us (25%)
  starting transfers between devices  26.3 us (16%)
  local copies, waits for them, and re-layouts  9.06 us (5%)
    pallas_call x4, Pallas kernels, chunk_call(): pl.pallas_call(functools.partial(chunk_kernel, first, last, held, chunk,...  45.1 us
    pallas_call x3, Pallas kernels, left_call(): pl.pallas_call(functools.partial(left_kernel, first, held, items, len(pay...  27.2 us
    ppermute x12, waiting for transfers between devices, gather(): moved.append(lax.ppermute(own, 'sec', pairs))  25.1 us
    ppermute x12, starting transfers between devices, gather(): moved.append(lax.ppermute(own, 'sec', pairs))  16.5 us
    ppermute x14, waiting for transfers between devices, swap(): return lax.ppermute(value, axis, [(i, i ^ bits) for i in range(size)])  16.1 us
    ppermute x14, starting transfers between devices, swap(): return lax.ppermute(value, axis, [(i, i ^ bits) for i in range(size)])  9.85 us
    unnamed x36, local copies, waits for them, and re-layouts  8.46 us
    pallas_call x1, Pallas kernels, residual_call(): pl.pallas_call(functools.partial(residual_kernel, sectors // 2, slots), i...  6.6 us
  transfers between devices with their start and end apart: 26, of which 13 were waited for; matrix products, arithmetic and copies ran while one was open for 0% of the time, Pallas kernels for 39%

profile of v2, /device:TPU:0, one launch (start us, length us, event | category | flops | bytes accessed | tf_op | source)
XLA Modules:
  0.0 166.9 jit_solution(16953104803100083227)
XLA Ops:
  2.4 3.7 %pack.1 = (bf16[2112,128]{1,0:T(8,128)(2,1)}, bf16[2112,128]{1,0:T(8,128)(2,1)}, bf16[8,1,128,128]{3,2,1,0:T(8,128)(2,1)}, bf16[8,1,128,128]{3,2,1,0:T(8,128)(2,...) custom-call(s32[8]{0:T(128)} %dynamic_slice.8.places, s32[4]{0:T(128)} %term_op.1, ...), custom_call_target="tpu_custom_call" | custom-call | bytes 2097152 | tf_op jit(solution)/shard_map/pack/pallas_call | solution.py:145
  6.7 1.8 %collective-permute-done.received_ref.rest_3_.rest_1_ = bf16[2112,128]{1,0:T(8,128)(2,1)S(1)} collective-permute-done((bf16[2112,128]{1,0:T(8,128)(2,1)}, bf16[2112,128]{1,0:T(8,128)(2,1)S(1)}, u32[]{:S(2)}, u32[]{:S(2)}) %collective-permute-start) | collective-permute-done | bytes 540704 | tf_op jit(solution)/shard_map/ppermute | solution.py:571
  9.6 2.9 %collective-permute-start.5 = (bf16[2,2112,128]{2,1,0:T(8,128)(2,1)S(1)}, bf16[2,2112,128]{2,1,0:T(8,128)(2,1)S(1)}, u32[]{:S(2)}, u32[]{:S(2)}) collective-permute-start(bf16[2,2112,128]{2,1,0:T(8,128)(2,1)S(1)} %stack.25.rest_0_), channel_id=1, source_target_pairs={{0,2},{1,3},{2,0},{3,1},{4,6},{5,7},{6,4},{7,5},{8,10},{9,11},{10,... | collective-permute-start | bytes 3244040 | tf_op jit(solution)/shard_map/ppermute | solution.py:571
  12.5 3.6 %collective-permute-start.3 = (bf16[8,1,128,128]{3,2,1,0:T(8,128)(2,1)}, bf16[8,1,128,128]{3,2,1,0:T(8,128)(2,1)S(1)}, u32[]{:S(2)}, u32[]{:S(2)}) collective-permute-start(bf16[8,1,128,128]{3,2,1,0:T(8,128)(2,1)} %get-tuple-element.44.rest_1_), channel_id=1, source_target_pairs={{0,12},{4,0},{8,4},{12,8},{1,13},{5,1},{9,5},{13,9},{2,14},{6,2},{... | collective-permute-start | bytes 786440 | tf_op jit(solution)/shard_map/ppermute | solution.py:594
  18.4 12.3 %left.3 = (bf16[8,1,8,256,128]{4,3,2,1,0:T(8,128)(2,1)S(1)}, bf16[8,1,8,256,128]{4,3,2,1,0:T(8,128)(2,1)S(1)}, bf16[8,1,8,256,128]{4,3,2,1,0:T(8,128)(2,1)S(1)},...) custom-call(s32[4]{0:T(128)S(1)} %pad_add_fusion.meta, ...), custom_call_target="tpu_custom_call" | custom-call | flops 25165824 | bytes 16384 | tf_op jit(solution)/shard_map/left/pallas_call | solution.py:257
  30.7 2.0 %copy-done.2 = bf16[8,1,8,256,128]{4,3,2,1,0:T(8,128)(2,1)} copy-done((bf16[8,1,8,256,128]{4,3,2,1,0:T(8,128)(2,1)}, bf16[8,1,8,256,128]{4,3,2,1,0:T(8,128)(2,1)S(1)}, u32[]{:S(2)}) %copy-start.2) | copy-done | bytes 4194328
  32.7 6.0 %collective-permute-done.2.rest_3_ = bf16[8,1,128,128]{3,2,1,0:T(8,128)(2,1)S(1)} collective-permute-done((bf16[8,1,128,128]{3,2,1,0:T(8,128)(2,1)}, bf16[8,1,128,128]{3,2,1,0:T(8,128)(2,1)S(1)}, u32[]{:S(2)}, u32[]{:S(2)}) %collective-permute-start.2) | collective-permute-done | bytes 262176 | tf_op jit(solution)/shard_map/ppermute | solution.py:594
  40.0 1.5 collective-permute-done.4.received_ref.rest_4_
  42.2 2.8 %collective-permute-start.8 = (bf16[8,1,128,128]{3,2,1,0:T(8,128)(2,1)S(1)}, bf16[8,1,128,128]{3,2,1,0:T(8,128)(2,1)S(1)}, u32[]{:S(2)}, u32[]{:S(2)}) collective-permute-start(bf16[8,1,128,128]{3,2,1,0:T(8,128)(2,1)S(1)} %copy-done.13), channel_id=1, source_target_pairs={{0,8},{4,12},{8,0},{12,4},{1,9},{5,13},{9,1},{13,5},{2,10},{6,14},... | collective-permute-start | bytes 786440 | tf_op jit(solution)/shard_map/ppermute | solution.py:594
  45.0 2.0 %collective-permute-start.7 = (bf16[8,1,128,128]{3,2,1,0:T(8,128)(2,1)S(1)}, bf16[8,1,128,128]{3,2,1,0:T(8,128)(2,1)S(1)}, u32[]{:S(2)}, u32[]{:S(2)}) collective-permute-start(bf16[8,1,128,128]{3,2,1,0:T(8,128)(2,1)S(1)} %copy-done.13), channel_id=1, source_target_pairs={{0,4},{4,8},{8,12},{12,0},{1,5},{5,9},{9,13},{13,1},{2,6},{6,10},{... | collective-permute-start | bytes 786440 | tf_op jit(solution)/shard_map/ppermute | solution.py:594
  47.0 8.4 %left.4 = (bf16[8,1,8,256,128]{4,3,2,1,0:T(8,128)(2,1)S(1)}, bf16[8,1,8,256,128]{4,3,2,1,0:T(8,128)(2,1)S(1)}, bf16[8,1,8,256,128]{4,3,2,1,0:T(8,128)(2,1)S(1)}, f32[8,128]{1,0:T(8,128)S(1)}) custom-call(s32[4]{0:T(128)S(1)} %pad_add_fusion.meta, s32[8]{0:T(128)S(1)} %select_reduce_fusion.places, s32[32]{0:T(128)S(1)} %copy-done.15, ...), custom_call_target="tpu_custom_call" | custom-call | flops 9437184 | bytes 8192 | tf_op jit(solution)/shard_map/left/pallas_call | solution.py:257
  55.4 2.0 %copy-done.6 = bf16[8,1,8,256,128]{4,3,2,1,0:T(8,128)(2,1)} copy-done((bf16[8,1,8,256,128]{4,3,2,1,0:T(8,128)(2,1)}, bf16[8,1,8,256,128]{4,3,2,1,0:T(8,128)(2,1)S(1)}, u32[]{:S(2)}) %copy-start.6) | copy-done | bytes 4194328
  57.5 10.7 %collective-permute-done.8.rest_4_ = bf16[8,1,128,128]{3,2,1,0:T(8,128)(2,1)S(1)} collective-permute-done((bf16[8,1,128,128]{3,2,1,0:T(8,128)(2,1)S(1)}, bf16[8,1,128,128]{3,2,1,0:T(8,128)(2,1)S(1)}, u32[]{:S(2)}, u32[]{:S(2)}) %collective-permute-start.8) | collective-permute-done | bytes 262176 | tf_op jit(solution)/shard_map/ppermute | solution.py:594
  71.1 1.6 collective-permute-start.11
  72.8 2.0 %collective-permute-start.12 = (bf16[8,1,128,128]{3,2,1,0:T(8,128)(2,1)S(1)}, bf16[8,1,128,128]{3,2,1,0:T(8,128)(2,1)S(1)}, u32[]{:S(2)}, u32[]{:S(2)}) collective-permute-start(bf16[8,1,128,128]{3,2,1,0:T(8,128)(2,1)S(1)} %copy-done.12), channel_id=1, source_target_pairs={{0,4},{4,8},{8,12},{12,0},{1,5},{5,9},{9,13},{13,1},{2,6},{6,10},{... | collective-permute-start | bytes 786440 | tf_op jit(solution)/shard_map/ppermute | solution.py:594
  74.9 2.2 %copy-done.3 = bf16[8,1,8,256,128]{4,3,2,1,0:T(8,128)(2,1)S(1)} copy-done((bf16[8,1,8,256,128]{4,3,2,1,0:T(8,128)(2,1)S(1)}, bf16[8,1,8,256,128]{4,3,2,1,0:T(8,128)(2,1)}, u32[]{:S(2)}) %copy-start.3) | copy-done | bytes 4194328
  77.0 13.2 %chunk.4 = (f32[8,16,128,128]{3,2,1,0:T(8,128)S(1)}, f32[8,128]{1,0:T(8,128)S(1)}) custom-call(s32[4]{0:T(128)S(1)} %pad_add_fusion.meta, s32[8]{0:T(128)S(1)} %select_reduce_fusion.places, s32[32]{0:T(128)S(1)} %copy-done.15, s32[8,2]{1,0:T(8,128)S(1)} %copy.35.partners, s32[8]{0:T(128)S(1)} %copy-done.14, ...), custom_call_target="tpu_custom_call" | custom-call | flops 13631488 | bytes 8192 | tf_op jit(solution)/shard_map/chunk/pallas_call | solution.py:447
  90.3 5.7 %collective-permute-done.13.rest_4_ = bf16[8,1,128,128]{3,2,1,0:T(8,128)(2,1)S(1)} collective-permute-done((bf16[8,1,128,128]{3,2,1,0:T(8,128)(2,1)S(1)}, bf16[8,1,128,128]{3,2,1,0:T(8,128)(2,1)S(1)}, u32[]{:S(2)}, u32[]{:S(2)}) %collective-permute-start.13) | collective-permute-done | bytes 262176 | tf_op jit(solution)/shard_map/ppermute | solution.py:594
  97.4 1.5 collective-permute-done.15.received_ref.rest_4_
  99.5 2.8 %collective-permute-start.18 = (bf16[8,1,128,128]{3,2,1,0:T(8,128)(2,1)S(1)}, bf16[8,1,128,128]{3,2,1,0:T(8,128)(2,1)S(1)}, u32[]{:S(2)}, u32[]{:S(2)}) collective-permute-start(bf16[8,1,128,128]{3,2,1,0:T(8,128)(2,1)S(1)} %copy-done.11), channel_id=1, source_target_pairs={{0,8},{4,12},{8,0},{12,4},{1,9},{5,13},{9,1},{13,5},{2,10},{6,14},... | collective-permute-start | bytes 786440 | tf_op jit(solution)/shard_map/ppermute | solution.py:594
  102.3 2.0 %collective-permute-start.17 = (bf16[8,1,128,128]{3,2,1,0:T(8,128)(2,1)S(1)}, bf16[8,1,128,128]{3,2,1,0:T(8,128)(2,1)S(1)}, u32[]{:S(2)}, u32[]{:S(2)}) collective-permute-start(bf16[8,1,128,128]{3,2,1,0:T(8,128)(2,1)S(1)} %copy-done.11), channel_id=1, source_target_pairs={{0,4},{4,8},{8,12},{12,0},{1,5},{5,9},{9,13},{13,1},{2,6},{6,10},{... | collective-permute-start | bytes 786440 | tf_op jit(solution)/shard_map/ppermute | solution.py:594
  104.4 11.9 %chunk.5 = (f32[8,16,128,128]{3,2,1,0:T(8,128)S(1)}, f32[8,128]{1,0:T(8,128)S(1)}) custom-call(s32[4]{0:T(128)S(1)} %pad_add_fusion.meta, s32[8]{0:T(128)S(1)} %select_reduce_fusion.places, s32[32]{0:T(128)S(1)} %copy-done.15, s32[8,2]{1,0:T(8,128)S(1)} %copy.35.partners, s32[8]{0:T(128)S(1)} %copy-done.14, ...), custom_call_target="tpu_custom_call", output_to_operand_aliasing={{0}: (13, {})} | custom-call | flops 10485760 | bytes 8192 | tf_op jit(solution)/shard_map/chunk/pallas_call | solution.py:447
  116.3 6.5 %left.5 = (bf16[8,1,8,256,128]{4,3,2,1,0:T(8,128)(2,1)S(1)}, bf16[8,1,8,256,128]{4,3,2,1,0:T(8,128)(2,1)S(1)}, f32[8,128]{1,0:T(8,128)S(1)}) custom-call(s32[4]{0:T(128)S(1)} %pad_add_fusion.meta, s32[8]{0:T(128)S(1)} %select_reduce_fusion.places, s32[32]{0:T(128)S(1)} %copy-done.15, s32[8,2]{1,0:T(8,128)S(1)} %copy.35.partners, s32[8]{0:T(128)S(1)} %copy-done.14, ...), custom_call_target="tpu_custom_call" | custom-call | flops 6291456 | bytes 8192 | tf_op jit(solution)/shard_map/left/pallas_call | solution.py:257
  122.9 2.6 %collective-permute-done.18.rest_4_ = bf16[8,1,128,128]{3,2,1,0:T(8,128)(2,1)S(1)} collective-permute-done((bf16[8,1,128,128]{3,2,1,0:T(8,128)(2,1)S(1)}, bf16[8,1,128,128]{3,2,1,0:T(8,128)(2,1)S(1)}, u32[]{:S(2)}, u32[]{:S(2)}) %collective-permute-start.18) | collective-permute-done | bytes 262176 | tf_op jit(solution)/shard_map/ppermute | solution.py:594
  126.9 1.5 collective-permute-done.20.received_ref.rest_5_
  128.4 1.6 collective-permute-start.21
  130.0 11.9 %chunk.6 = (f32[8,16,128,128]{3,2,1,0:T(8,128)S(1)}, f32[8,128]{1,0:T(8,128)S(1)}) custom-call(s32[4]{0:T(128)S(1)} %pad_add_fusion.meta, s32[8]{0:T(128)S(1)} %select_reduce_fusion.places, s32[32]{0:T(128)S(1)} %copy-done.15, s32[8,2]{1,0:T(8,128)S(1)} %copy.35.partners, s32[8]{0:T(128)S(1)} %copy-done.14, ...), custom_call_target="tpu_custom_call", output_to_operand_aliasing={{0}: (13, {})} | custom-call | flops 10485760 | bytes 8192 | tf_op jit(solution)/shard_map/chunk/pallas_call | solution.py:447
  142.5 8.1 %chunk.7 = (bf16[8,16,128,128]{3,2,1,0:T(8,128)(2,1)S(1)}, f32[8,128]{1,0:T(8,128)S(1)}) custom-call(s32[4]{0:T(128)S(1)} %pad_add_fusion.meta, s32[8]{0:T(128)S(1)} %select_reduce_fusion.places, s32[32]{0:T(128)S(1)} %copy-done.15, s32[8,2]{1,0:T(8,128)S(1)} %copy.35.partners, s32[8]{0:T(128)S(1)} %copy-done.14, f32[8,128]{1,0:T(8,128)S(1)} %get-tuple-element.71.after_ref, ...), custom_call_target="tpu_custom_call" | custom-call | flops 4194304 | bytes 8192 | tf_op jit(solution)/shard_map/chunk/pallas_call | solution.py:447
  150.7 3.6 %collective-permute-done.22 = f32[16,128]{1,0:T(8,128)S(1)} collective-permute-done((f32[16,128]{1,0:T(8,128)S(1)}, f32[16,128]{1,0:T(8,128)S(1)}, u32[]{:S(2)}, u32[]{:S(2)}) %collective-permute-start.22) | collective-permute-done | bytes 8224 | tf_op jit(solution)/shard_map/ppermute | solution.py:571
  154.4 1.7 collective-permute-start.23
  156.0 2.9 %collective-permute-done.23 = f32[16,128]{1,0:T(8,128)S(1)} collective-permute-done((f32[16,128]{1,0:T(8,128)S(1)}, f32[16,128]{1,0:T(8,128)S(1)}, u32[]{:S(2)}, u32[]{:S(2)}) %collective-permute-start.23) | collective-permute-done | bytes 8224 | tf_op jit(solution)/shard_map/ppermute | solution.py:571
  160.1 6.6 %residual.1 = (bf16[8,2,16,128,128]{4,3,2,1,0:T(8,128)(2,1)}, f32[1]{0:T(128)}) custom-call(s32[4]{0:T(128)S(1)} %pad_add_fusion.meta, s32[8]{0:T(128)S(1)} %select_reduce_fusion.places, s32[32]{0:T(128)S(1)} %copy-done.15, s32[8,2]{1,0:T(8,128)S(1)} %copy.35.partners, s32[8]{0:T(128)S(1)} %copy-done.14, f32[16,128]{1,0:T(8,128)S(1)} %add.44.folds_ref, ...), custom_call_target="tpu_custom_call" | custom-call | flops 12582912 | bytes 25165824 | tf_op jit(solution)/shard_map/residual/pallas_call | solution.py:525
  (85 shorter events, 16.0 us)
Async XLA Ops:
  6.2 2.3 %collective-permute-start = (bf16[2112,128]{1,0:T(8,128)(2,1)}, bf16[2112,128]{1,0:T(8,128)(2,1)S(1)}, u32[]{:S(2)}, u32[]{:S(2)}) collective-permute-start(bf16[2112,128]{1,0:T(8,128)(2,1)} %get-tuple-element.42), channel_id=1, source_target_pairs={{0,1},{1,0},{2,3},{3,2},{4,5},{5,4},{6,7},{7,6},{8,9},{9,8},{10,11... | collective-permute-start | bytes 1622024 | tf_op jit(solution)/shard_map/ppermute | solution.py:571
  9.6 37.4 %collective-permute-start.5 = (bf16[2,2112,128]{2,1,0:T(8,128)(2,1)S(1)}, bf16[2,2112,128]{2,1,0:T(8,128)(2,1)S(1)}, u32[]{:S(2)}, u32[]{:S(2)}) collective-permute-start(bf16[2,2112,128]{2,1,0:T(8,128)(2,1)S(1)} %stack.25.rest_0_), channel_id=1, source_target_pairs={{0,2},{1,3},{2,0},{3,1},{4,6},{5,7},{6,4},{7,5},{8,10},{9,11},{10,... | collective-permute-start | bytes 3244040 | tf_op jit(solution)/shard_map/ppermute | solution.py:571
  12.5 20.2 %collective-permute-start.3 = (bf16[8,1,128,128]{3,2,1,0:T(8,128)(2,1)}, bf16[8,1,128,128]{3,2,1,0:T(8,128)(2,1)S(1)}, u32[]{:S(2)}, u32[]{:S(2)}) collective-permute-start(bf16[8,1,128,128]{3,2,1,0:T(8,128)(2,1)} %get-tuple-element.44.rest_1_), channel_id=1, source_target_pairs={{0,12},{4,0},{8,4},{12,8},{1,13},{5,1},{9,5},{13,9},{2,14},{6,2},{... | collective-permute-start | bytes 786440 | tf_op jit(solution)/shard_map/ppermute | solution.py:594
  16.1 22.5 %collective-permute-start.2 = (bf16[8,1,128,128]{3,2,1,0:T(8,128)(2,1)}, bf16[8,1,128,128]{3,2,1,0:T(8,128)(2,1)S(1)}, u32[]{:S(2)}, u32[]{:S(2)}) collective-permute-start(bf16[8,1,128,128]{3,2,1,0:T(8,128)(2,1)} %get-tuple-element.44.rest_1_), channel_id=1, source_target_pairs={{0,8},{4,12},{8,0},{12,4},{1,9},{5,13},{9,1},{13,5},{2,10},{6,14},... | collective-permute-start | bytes 786440 | tf_op jit(solution)/shard_map/ppermute | solution.py:594
  16.1 22.5 %collective-permute-start.1 = (bf16[8,1,128,128]{3,2,1,0:T(8,128)(2,1)}, bf16[8,1,128,128]{3,2,1,0:T(8,128)(2,1)S(1)}, u32[]{:S(2)}, u32[]{:S(2)}) collective-permute-start(bf16[8,1,128,128]{3,2,1,0:T(8,128)(2,1)} %get-tuple-element.44.rest_1_), channel_id=1, source_target_pairs={{0,4},{4,8},{8,12},{12,0},{1,5},{5,9},{9,13},{13,1},{2,6},{6,10},{... | collective-permute-start | bytes 786440 | tf_op jit(solution)/shard_map/ppermute | solution.py:594
  18.4 23.8 %copy-start.13 = (bf16[8,1,128,128]{3,2,1,0:T(8,128)(2,1)S(1)}, bf16[8,1,128,128]{3,2,1,0:T(8,128)(2,1)}, u32[]{:S(2)}) copy-start(bf16[8,1,128,128]{3,2,1,0:T(8,128)(2,1)} %get-tuple-element.50.rest_2_) | copy-start | bytes 786436
  32.7 22.7 %copy-start = (bf16[8,1,8,256,128]{4,3,2,1,0:T(8,128)(2,1)}, bf16[8,1,8,256,128]{4,3,2,1,0:T(8,128)(2,1)S(1)}, u32[]{:S(2)}) copy-start(bf16[8,1,8,256,128]{4,3,2,1,0:T(8,128)(2,1)S(1)} %get-tuple-element.59.rest_0_) | copy-start | bytes 12582916
  32.7 22.7 %copy-start.4 = (bf16[8,1,8,256,128]{4,3,2,1,0:T(8,128)(2,1)}, bf16[8,1,8,256,128]{4,3,2,1,0:T(8,128)(2,1)S(1)}, u32[]{:S(2)}) copy-start(bf16[8,1,8,256,128]{4,3,2,1,0:T(8,128)(2,1)S(1)} %get-tuple-element.72.rest_0_) | copy-start | bytes 12582916
  40.0 1.6 collective-permute-start.4
  41.6 26.6 %collective-permute-start.6 = (bf16[2,8,1,128,128]{4,3,2,1,0:T(8,128)(2,1)S(1)}, bf16[2,8,1,128,128]{4,3,2,1,0:T(8,128)(2,1)S(1)}, u32[]{:S(2)}, u32[]{:S(2)}) collective-permute-start(bf16[2,8,1,128,128]{4,3,2,1,0:T(8,128)(2,1)S(1)} %stack.26.rest_0_), channel_id=1, source_target_pairs={{0,2},{1,3},{2,0},{3,1},{4,6},{5,7},{6,4},{7,5},{8,10},{9,11},{10,... | collective-permute-start | bytes 1572872 | tf_op jit(solution)/shard_map/ppermute | solution.py:571
  42.2 15.3 %collective-permute-start.9 = (bf16[8,1,128,128]{3,2,1,0:T(8,128)(2,1)S(1)}, bf16[8,1,128,128]{3,2,1,0:T(8,128)(2,1)S(1)}, u32[]{:S(2)}, u32[]{:S(2)}) collective-permute-start(bf16[8,1,128,128]{3,2,1,0:T(8,128)(2,1)S(1)} %copy-done.13), channel_id=1, source_target_pairs={{0,12},{4,0},{8,4},{12,8},{1,13},{5,1},{9,5},{13,9},{2,14},{6,2},{... | collective-permute-start | bytes 786440 | tf_op jit(solution)/shard_map/ppermute | solution.py:594
  42.2 26.0 %collective-permute-start.8 = (bf16[8,1,128,128]{3,2,1,0:T(8,128)(2,1)S(1)}, bf16[8,1,128,128]{3,2,1,0:T(8,128)(2,1)S(1)}, u32[]{:S(2)}, u32[]{:S(2)}) collective-permute-start(bf16[8,1,128,128]{3,2,1,0:T(8,128)(2,1)S(1)} %copy-done.13), channel_id=1, source_target_pairs={{0,8},{4,12},{8,0},{12,4},{1,9},{5,13},{9,1},{13,5},{2,10},{6,14},... | collective-permute-start | bytes 786440 | tf_op jit(solution)/shard_map/ppermute | solution.py:594
  45.0 23.2 %collective-permute-start.7 = (bf16[8,1,128,128]{3,2,1,0:T(8,128)(2,1)S(1)}, bf16[8,1,128,128]{3,2,1,0:T(8,128)(2,1)S(1)}, u32[]{:S(2)}, u32[]{:S(2)}) collective-permute-start(bf16[8,1,128,128]{3,2,1,0:T(8,128)(2,1)S(1)} %copy-done.13), channel_id=1, source_target_pairs={{0,4},{4,8},{8,12},{12,0},{1,5},{5,9},{9,13},{13,1},{2,6},{6,10},{... | collective-permute-start | bytes 786440 | tf_op jit(solution)/shard_map/ppermute | solution.py:594
  47.0 25.6 %copy-start.12 = (bf16[8,1,128,128]{3,2,1,0:T(8,128)(2,1)S(1)}, bf16[8,1,128,128]{3,2,1,0:T(8,128)(2,1)}, u32[]{:S(2)}) copy-start(bf16[8,1,128,128]{3,2,1,0:T(8,128)(2,1)} %get-tuple-element.56.rest_2_) | copy-start | bytes 786436
  69.5 1.6 collective-permute-start.10
  71.1 24.9 %collective-permute-start.11 = (bf16[2,8,1,128,128]{4,3,2,1,0:T(8,128)(2,1)S(1)}, bf16[2,8,1,128,128]{4,3,2,1,0:T(8,128)(2,1)S(1)}, u32[]{:S(2)}, u32[]{:S(2)}) collective-permute-start(bf16[2,8,1,128,128]{4,3,2,1,0:T(8,128)(2,1)S(1)} %stack.27.after_ref), channel_id=1, source_target_pairs={{0,2},{1,3},{2,0},{3,1},{4,6},{5,7},{6,4},{7,5},{8,10},{9,11},{10,... | collective-permute-start | bytes 1572872 | tf_op jit(solution)/shard_map/ppermute | solution.py:571
  72.7 17.6 %collective-permute-start.14 = (bf16[8,1,128,128]{3,2,1,0:T(8,128)(2,1)S(1)}, bf16[8,1,128,128]{3,2,1,0:T(8,128)(2,1)S(1)}, u32[]{:S(2)}, u32[]{:S(2)}) collective-permute-start(bf16[8,1,128,128]{3,2,1,0:T(8,128)(2,1)S(1)} %copy-done.12), channel_id=1, source_target_pairs={{0,12},{4,0},{8,4},{12,8},{1,13},{5,1},{9,5},{13,9},{2,14},{6,2},{... | collective-permute-start | bytes 786440 | tf_op jit(solution)/shard_map/ppermute | solution.py:594
  72.7 23.3 %collective-permute-start.13 = (bf16[8,1,128,128]{3,2,1,0:T(8,128)(2,1)S(1)}, bf16[8,1,128,128]{3,2,1,0:T(8,128)(2,1)S(1)}, u32[]{:S(2)}, u32[]{:S(2)}) collective-permute-start(bf16[8,1,128,128]{3,2,1,0:T(8,128)(2,1)S(1)} %copy-done.12), channel_id=1, source_target_pairs={{0,8},{4,12},{8,0},{12,4},{1,9},{5,13},{9,1},{13,5},{2,10},{6,14},... | collective-permute-start | bytes 786440 | tf_op jit(solution)/shard_map/ppermute | solution.py:594
  72.8 23.2 %collective-permute-start.12 = (bf16[8,1,128,128]{3,2,1,0:T(8,128)(2,1)S(1)}, bf16[8,1,128,128]{3,2,1,0:T(8,128)(2,1)S(1)}, u32[]{:S(2)}, u32[]{:S(2)}) collective-permute-start(bf16[8,1,128,128]{3,2,1,0:T(8,128)(2,1)S(1)} %copy-done.12), channel_id=1, source_target_pairs={{0,4},{4,8},{8,12},{12,0},{1,5},{5,9},{9,13},{13,1},{2,6},{6,10},{... | collective-permute-start | bytes 786440 | tf_op jit(solution)/shard_map/ppermute | solution.py:594
  77.0 22.5 %copy-start.11 = (bf16[8,1,128,128]{3,2,1,0:T(8,128)(2,1)S(1)}, bf16[8,1,128,128]{3,2,1,0:T(8,128)(2,1)}, u32[]{:S(2)}) copy-start(bf16[8,1,128,128]{3,2,1,0:T(8,128)(2,1)} %get-tuple-element.65.rest_2_) | copy-start | bytes 786436
  77.0 27.3 %copy-start.1 = (bf16[8,1,8,256,128]{4,3,2,1,0:T(8,128)(2,1)S(1)}, bf16[8,1,8,256,128]{4,3,2,1,0:T(8,128)(2,1)}, u32[]{:S(2)}) copy-start(bf16[8,1,8,256,128]{4,3,2,1,0:T(8,128)(2,1)} %copy-done) | copy-start | bytes 12582916
  97.3 1.6 collective-permute-start.15
  98.9 26.6 %collective-permute-start.16 = (bf16[2,8,1,128,128]{4,3,2,1,0:T(8,128)(2,1)S(1)}, bf16[2,8,1,128,128]{4,3,2,1,0:T(8,128)(2,1)S(1)}, u32[]{:S(2)}, u32[]{:S(2)}) collective-permute-start(bf16[2,8,1,128,128]{4,3,2,1,0:T(8,128)(2,1)S(1)} %stack.28.after_ref), channel_id=1, source_target_pairs={{0,2},{1,3},{2,0},{3,1},{4,6},{5,7},{6,4},{7,5},{8,10},{9,11},{10,... | collective-permute-start | bytes 1572872 | tf_op jit(solution)/shard_map/ppermute | solution.py:571
  99.5 23.3 %collective-permute-start.19 = (bf16[8,1,128,128]{3,2,1,0:T(8,128)(2,1)S(1)}, bf16[8,1,128,128]{3,2,1,0:T(8,128)(2,1)S(1)}, u32[]{:S(2)}, u32[]{:S(2)}) collective-permute-start(bf16[8,1,128,128]{3,2,1,0:T(8,128)(2,1)S(1)} %copy-done.11), channel_id=1, source_target_pairs={{0,12},{4,0},{8,4},{12,8},{1,13},{5,1},{9,5},{13,9},{2,14},{6,2},{... | collective-permute-start | bytes 786440 | tf_op jit(solution)/shard_map/ppermute | solution.py:594
  99.5 26.0 %collective-permute-start.18 = (bf16[8,1,128,128]{3,2,1,0:T(8,128)(2,1)S(1)}, bf16[8,1,128,128]{3,2,1,0:T(8,128)(2,1)S(1)}, u32[]{:S(2)}, u32[]{:S(2)}) collective-permute-start(bf16[8,1,128,128]{3,2,1,0:T(8,128)(2,1)S(1)} %copy-done.11), channel_id=1, source_target_pairs={{0,8},{4,12},{8,0},{12,4},{1,9},{5,13},{9,1},{13,5},{2,10},{6,14},... | collective-permute-start | bytes 786440 | tf_op jit(solution)/shard_map/ppermute | solution.py:594
  102.3 23.2 %collective-permute-start.17 = (bf16[8,1,128,128]{3,2,1,0:T(8,128)(2,1)S(1)}, bf16[8,1,128,128]{3,2,1,0:T(8,128)(2,1)S(1)}, u32[]{:S(2)}, u32[]{:S(2)}) collective-permute-start(bf16[8,1,128,128]{3,2,1,0:T(8,128)(2,1)S(1)} %copy-done.11), channel_id=1, source_target_pairs={{0,4},{4,8},{8,12},{12,0},{1,5},{5,9},{9,13},{13,1},{2,6},{6,10},{... | collective-permute-start | bytes 786440 | tf_op jit(solution)/shard_map/ppermute | solution.py:594
  126.8 1.6 collective-permute-start.20
  128.4 14.0 %collective-permute-start.21 = (bf16[2,8,1,128,128]{4,3,2,1,0:T(8,128)(2,1)S(1)}, bf16[2,8,1,128,128]{4,3,2,1,0:T(8,128)(2,1)S(1)}, u32[]{:S(2)}, u32[]{:S(2)}) collective-permute-start(bf16[2,8,1,128,128]{4,3,2,1,0:T(8,128)(2,1)S(1)} %stack.29.after_ref), channel_id=1, source_target_pairs={{0,2},{1,3},{2,0},{3,1},{4,6},{5,7},{6,4},{7,5},{8,10},{9,11},{10,... | collective-permute-start | bytes 1572872 | tf_op jit(solution)/shard_map/ppermute | solution.py:571
  150.6 9.6 %collective-permute-start.25 = (bf16[8,16,128,128]{3,2,1,0:T(8,128)(2,1)S(1)}, bf16[8,16,128,128]{3,2,1,0:T(8,128)(2,1)S(1)}, u32[]{:S(2)}, u32[]{:S(2)}) collective-permute-start(bf16[8,16,128,128]{3,2,1,0:T(8,128)(2,1)S(1)} %get-tuple-element.79.own_ref), channel_id=1, source_target_pairs={{0,1},{1,0},{2,3},{3,2},{4,5},{5,4},{6,7},{7,6},{8,9},{9,8},{10,11... | collective-permute-start | bytes 12582920 | tf_op jit(solution)/shard_map/ppermute | solution.py:571
  150.7 3.7 %collective-permute-start.22 = (f32[16,128]{1,0:T(8,128)S(1)}, f32[16,128]{1,0:T(8,128)S(1)}, u32[]{:S(2)}, u32[]{:S(2)}) collective-permute-start(f32[16,128]{1,0:T(8,128)S(1)} %constant_dynamic-update-slice_fusion), channel_id=1, source_target_pairs={{0,4},{4,0},{8,12},{12,8},{1,5},{5,1},{9,13},{13,9},{2,6},{6,2},{1... | collective-permute-start | bytes 24584 | tf_op jit(solution)/shard_map/ppermute | solution.py:571
  154.4 4.5 %collective-permute-start.23 = (f32[16,128]{1,0:T(8,128)S(1)}, f32[16,128]{1,0:T(8,128)S(1)}, u32[]{:S(2)}, u32[]{:S(2)}) collective-permute-start(f32[16,128]{1,0:T(8,128)S(1)} %add.42), channel_id=1, source_target_pairs={{0,8},{4,12},{8,0},{12,4},{1,9},{5,13},{9,1},{13,5},{2,10},{6,14},... | collective-permute-start | bytes 24584 | tf_op jit(solution)/shard_map/ppermute | solution.py:571
  158.9 1.2 collective-permute-start.24
  (11 other events, 103.4 us)

commit v3 on v2

--- a/solution.py
+++ b/solution.py
@@ -280,55 +280,57 @@
     )(*scalars, *afters, psi, *payloads)
 
 
-def stack_kernel(near_ref, received_ref, both_ref):
-    both_ref[0] = near_ref[...]
-    both_ref[1] = received_ref[...]
-
-
-def stack_call(near, received):
+def stack_kernel(start, near_ref, received_ref, both_ref):
+    terms = both_ref.shape[2] if len(both_ref.shape) == 5 else None
+    for side, ref in enumerate((near_ref, received_ref)):
+        both_ref[side] = ref[...] if start is None else ref[:, start : start + terms]
+
+
+def stack_call(near, received, chunk=None):
+    start, terms = chunk or (None, None)
+    shape = near.shape if chunk is None else (near.shape[0], terms) + near.shape[2:]
     return pl.pallas_call(
-        stack_kernel,
+        functools.partial(stack_kernel, start),
         in_specs=resident(2),
         out_specs=resident(1)[0],
-        out_shape=jax.ShapeDtypeStruct((2,) + near.shape, near.dtype),
+        out_shape=jax.ShapeDtypeStruct((2,) + shape, near.dtype),
         compiler_params=pltpu.CompilerParams(vmem_limit_bytes=SPARE),
-        cost_estimate=pl.CostEstimate(flops=0, bytes_accessed=8 * near.size, transcendentals=0),
+        cost_estimate=pl.CostEstimate(flops=0, bytes_accessed=4096, transcendentals=0),
         name="stack",
     )(near, received)
 
 
-def choose_kernel(devices, afters, sectors, half, slots, meta, places, partners, *rest):
+def choose_kernel(count, afters, half, slots, meta, places, partners, *rest):
     rest = rest[afters:]
-    shards, (mine_ref, other_ref) = rest[:devices], rest[devices:]
+    pieces, (mine_ref, other_ref) = rest[:count], rest[count:]
+    sectors = pieces[0].shape[1]
     for part, out_ref in enumerate((mine_ref, other_ref)):
         for block in range(half * slots):
             sector = places[(meta[1] ^ part) * half + block // slots]
             partner = partners[sector, block % slots]
-            away = lax.rem(meta[3] + devices - partner // sectors, devices)
+            away = meta[3] ^ (partner // sectors)
             place = lax.rem(partner, sectors)
-            for distance in range(devices):
-                @pl.when(away == distance)
-                def _(distance=distance, place=place, block=block, out_ref=out_ref):
-                    out_ref[block] = shards[distance][place]
-
-
-def choose_call(scalars, half, slots, shards, afters):
+            for at in range(count):
+                @pl.when(away // 2 == at)
+                def _(at=at, away=away, place=place, block=block, out_ref=out_ref):
+                    out_ref[block] = pieces[at][away & 1, place]
+
+
+def choose_call(scalars, half, slots, pieces, afters):
     meta, places, _, partners, _ = scalars
-    sectors, terms, width = shards[0].shape[:3]
+    terms, width = pieces[0].shape[2:4]
     chosen = jax.ShapeDtypeStruct((half * slots, terms, width, width), jnp.bfloat16)
     return pl.pallas_call(
-        functools.partial(choose_kernel, len(shards), len(afters), sectors, half, slots),
+        functools.partial(choose_kernel, len(pieces), len(afters), half, slots),
         in_specs=in_smem(3)
         + [pl.BlockSpec(memory_space=pl.ANY)] * len(afters)
-        + resident(len(shards)),
+        + resident(len(pieces)),
         out_specs=resident(2),
         out_shape=[chosen, chosen],
         compiler_params=pltpu.CompilerParams(vmem_limit_bytes=SPARE),
-        cost_estimate=pl.CostEstimate(
-            flops=0, bytes_accessed=8 * half * slots * terms * width * width, transcendentals=0
-        ),
+        cost_estimate=pl.CostEstimate(flops=0, bytes_accessed=4096, transcendentals=0),
         name="choose",
-    )(meta, places, partners, *afters, *shards)
+    )(meta, places, partners, *afters, *pieces)
 
 
 def chunk_kernel(first, last, held, chunk, ahead, late, count, half, slots,
@@ -576,23 +578,33 @@
 
     chunks = [(at, 1) for at in range(terms)]
     ordered = jnp.roll(places, -core * half)
+    parcels = [chunks[0], (chunks[0][1], terms - chunks[0][1])]
     mine, theirs, *shares = pack_call(
-        chunks, ordered, term_op, local_ops, left_env, right_env
+        parcels, ordered, term_op, local_ops, left_env, right_env
     )
     near_left = swap(theirs, 1)
     both_lefts, far_lefts = to_far_chips(mine, near_left)
 
     shards, rights = [], []
-
-    def gather(token):
-        own = shares[len(shards)]
+    swapped = [swap(share, 1, "sec", rings) for share in shares]
+
+    def gather(token=None):
+        at = len(shards)
+        if at == 0:
+            pair = stack_call(shares[0], swapped[0])
+        else:
+            start, length = chunks[at]
+            pair = stack_call(shares[1], swapped[1], (start - parcels[1][0], length))
+        sent = pair
         if token is not None:
-            own, _ = lax.optimization_barrier((own, token))
-        moved = [own]
-        for distance in range(1, rings):
-            pairs = [(i, (i + distance) % rings) for i in range(rings)]
-            moved.append(lax.ppermute(own, "sec", pairs))
-        shards.append(moved)
+            sent, _ = lax.optimization_barrier((pair, token))
+        pieces = [pair]
+        bits = 2
+        while bits < rings:
+            source = [sent] + pieces[1:]
+            pieces = pieces + [swap(piece, bits, "sec", rings) for piece in source]
+            bits *= 2
+        shards.append(pieces)
 
     def choose(token):
         afters = [token] + (rights[-1][2:] if rights else [])
@@ -622,18 +634,18 @@
         return outs[len(items) :]
 
     every = range(len(chunks))
-    gather(None)
+    gather()
     token, live_psi, squares = go_left((0,), every, both_lefts, True)
-    gather(token)
+    gather()
     token = choose(token)
     token, = go_left((1,), every[1:], token, waits=far_lefts)
     total = None
     for at, chunk in enumerate(chunks):
         last = at == len(chunks) - 1
+        if len(shards) < len(chunks):
+            gather(shards[at][-1])
         if len(rights) < len(chunks):
             token = choose(token)
-        if len(shards) < len(chunks):
-            gather(token)
         ahead = tuple(source for source in range(devices) if (at, source) in products)
         late = tuple(source for source in range(devices) if source not in ahead)
         payloads = ([near_left] if 1 in late else []) + (far_lefts if late else [])

time: 167 us -> 170 us (1.018)
  waiting for transfers between devices: 41.2 us -> 65 us
  Pallas kernels: 88 us -> 73.2 us
  starting transfers between devices: 26.3 us -> 20.3 us
    ppermute x14 -> x20, waiting for transfers between devices: 16.1 us -> 65 us  [swap(): return lax.ppermute(value, axis, [(i, i ^ bits) for i in range(size)])]
    ppermute x12 -> x0, waiting for transfers between devices: 25.1 us -> none  [gather(): moved.append(lax.ppermute(own, 'sec', pairs))]
    ppermute x12 -> x0, starting transfers between devices: 16.5 us -> none  [gather(): moved.append(lax.ppermute(own, 'sec', pairs))]
    ppermute x14 -> x20, starting transfers between devices: 9.85 us -> 20.3 us  [swap(): return lax.ppermute(value, axis, [(i, i ^ bits) for i in range(size)])]
    pallas_call x4, Pallas kernels: 45.1 us -> 34.9 us  [chunk_call(): pl.pallas_call(functools.partial(chunk_kernel, first, last, held, chunk,...]
    pallas_call x3, Pallas kernels: 27.2 us -> 21.3 us  [left_call(): pl.pallas_call(functools.partial(left_kernel, first, held, items, len(pay...]
    pallas_call x9 -> x13, Pallas kernels: 5.31 us -> 6.61 us  [the longest x4 5.47 us: choose_call(): pl.pallas_call(functools.partial(choose_kernel, len(pieces), len(afters),...]
    unnamed x36 -> x32, local copies, waits for them, and re-layouts: 8.46 us -> 7.18 us
  transfers between devices with their start and end apart: 26 -> 20, of which waited for: 13 -> 13; matrix products, arithmetic and copies ran while one was open for 0% -> 0% of each run, Pallas kernels for 39% -> 31%
where the time goes in v3:
time: 170 us; the launch traced here: 169 us
  Pallas kernels  73.2 us (43%)
  waiting for transfers between devices  65 us (38%)
  starting transfers between devices  20.3 us (12%)
  local copies, waits for them, and re-layouts  7.78 us (5%)
    ppermute x20, waiting for transfers between devices, swap(): return lax.ppermute(value, axis, [(i, i ^ bits) for i in range(size)])  65 us
    pallas_call x4, Pallas kernels, chunk_call(): pl.pallas_call(functools.partial(chunk_kernel, first, last, held, chunk,...  34.9 us
    pallas_call x3, Pallas kernels, left_call(): pl.pallas_call(functools.partial(left_kernel, first, held, items, len(pay...  21.3 us
    ppermute x20, starting transfers between devices, swap(): return lax.ppermute(value, axis, [(i, i ^ bits) for i in range(size)])  20.3 us
    unnamed x32, local copies, waits for them, and re-layouts  7.18 us
    pallas_call x1, Pallas kernels, residual_call(): pl.pallas_call(functools.partial(residual_kernel, sectors // 2, slots), i...  6.6 us
    pallas_call x4, Pallas kernels, choose_call(): pl.pallas_call(functools.partial(choose_kernel, len(pieces), len(afters),...  5.47 us
    pallas_call x1, Pallas kernels, pack_call(): pl.pallas_call(functools.partial(pack_kernel, chunks, half, terms), in_sp...  3.82 us
  transfers between devices with their start and end apart: 20, of which 13 were waited for; matrix products, arithmetic and copies ran while one was open for 0% of the time, Pallas kernels for 31%

profile of v3, /device:TPU:0, one launch (start us, length us, event | category | flops | bytes accessed | tf_op | source)
XLA Modules:
  0.0 168.7 jit_solution(14328601556577899818)
XLA Ops:
  2.4 3.8 %pack.1 = (bf16[2112,128]{1,0:T(8,128)(2,1)}, bf16[2112,128]{1,0:T(8,128)(2,1)}, bf16[8,1,128,128]{3,2,1,0:T(8,128)(2,1)}, bf16[8,3,128,128]{3,2,1,0:T(8,128)(2,1)}) custom-call(s32[8]{0:T(128)} %dynamic_slice.8.places, s32[4]{0:T(128)} %term_op.1, bf16[8,16,16]{2,1,0:T(8,128)(2,1)} %ops_ref.1, bf16[8,512,128]{2,1,0:T(8,128)(2,1)} %bitcast.5, ...), custom_call_target="tpu_custom_call" | custom-call | bytes 2097152 | tf_op jit(solution)/shard_map/pack/pallas_call | solution.py:145
  6.8 2.6 %collective-permute-start.1 = (bf16[8,1,128,128]{3,2,1,0:T(8,128)(2,1)}, bf16[8,1,128,128]{3,2,1,0:T(8,128)(2,1)S(1)}, u32[]{:S(2)}, u32[]{:S(2)}) collective-permute-start(bf16[8,1,128,128]{3,2,1,0:T(8,128)(2,1)} %get-tuple-element.41.near_ref), channel_id=1, source_target_pairs={{0,4},{4,0},{8,12},{12,8},{1,5},{5,1},{9,13},{13,9},{2,6},{6,2},{1... | collective-permute-start | bytes 786440 | tf_op jit(solution)/shard_map/ppermute | solution.py:573
  9.4 7.1 %collective-permute-done.1.received_ref = bf16[8,1,128,128]{3,2,1,0:T(8,128)(2,1)S(1)} collective-permute-done((bf16[8,1,128,128]{3,2,1,0:T(8,128)(2,1)}, bf16[8,1,128,128]{3,2,1,0:T(8,128)(2,1)S(1)}, u32[]{:S(2)}, u32[]{:S(2)}) %collective-permute-start.1) | collective-permute-done | bytes 262176 | tf_op jit(solution)/shard_map/ppermute | solution.py:573
  18.3 2.8 %collective-permute-start.2 = (bf16[2,8,1,128,128]{4,3,2,1,0:T(8,128)(2,1)}, bf16[2,8,1,128,128]{4,3,2,1,0:T(8,128)(2,1)}, u32[]{:S(2)}, u32[]{:S(2)}) collective-permute-start(bf16[2,8,1,128,128]{4,3,2,1,0:T(8,128)(2,1)} %stack.30.rest_1_), channel_id=1, source_target_pairs={{0,8},{4,12},{8,0},{12,4},{1,9},{5,13},{9,1},{13,5},{2,10},{6,14},... | collective-permute-start | bytes 1572872 | tf_op jit(solution)/shard_map/ppermute | solution.py:573
  21.1 1.6 collective-permute-start.6
  23.8 1.6 collective-permute-start.4
  26.6 9.6 %left.3 = (bf16[8,1,8,256,128]{4,3,2,1,0:T(8,128)(2,1)S(1)}, bf16[8,1,8,256,128]{4,3,2,1,0:T(8,128)(2,1)S(1)}, bf16[8,1,8,256,128]{4,3,2,1,0:T(8,128)(2,1)S(1)},...) custom-call(s32[4]{0:T(128)S(1)} %pad_add_fusion.meta, ...), custom_call_target="tpu_custom_call" | custom-call | flops 25165824 | bytes 16384 | tf_op jit(solution)/shard_map/left/pallas_call | solution.py:257
  36.2 2.0 %copy-done.3 = bf16[8,1,8,256,128]{4,3,2,1,0:T(8,128)(2,1)} copy-done((bf16[8,1,8,256,128]{4,3,2,1,0:T(8,128)(2,1)}, bf16[8,1,8,256,128]{4,3,2,1,0:T(8,128)(2,1)S(1)}, u32[]{:S(2)}) %copy-start.3) | copy-done | bytes 4194328
  38.2 6.3 %collective-permute-done.2.rest_2_ = bf16[2,8,1,128,128]{4,3,2,1,0:T(8,128)(2,1)} collective-permute-done((bf16[2,8,1,128,128]{4,3,2,1,0:T(8,128)(2,1)}, bf16[2,8,1,128,128]{4,3,2,1,0:T(8,128)(2,1)}, u32[]{:S(2)}, u32[]{:S(2)}) %collective-permute-start.2) | collective-permute-done | bytes 524320 | tf_op jit(solution)/shard_map/ppermute | solution.py:573
  44.6 1.8 %choose.4 = (bf16[8,1,128,128]{3,2,1,0:T(8,128)(2,1)S(1)}, bf16[8,1,128,128]{3,2,1,0:T(8,128)(2,1)S(1)}) custom-call(s32[4]{0:T(128)S(1)} %pad_add_fusion.meta, s32[8]{0:T(128)S(1)} %select_reduce_fusion.places, s32[8,2]{1,0:T(8,128)S(1)} %copy.35.partners, f32[8,128]{1,0:T(8,128)S(1)} %get-tuple-element.40.rest_0_, ...), custom_call_target="tpu_custom_call" | custom-call | bytes 4096 | tf_op jit(solution)/shard_map/choose/pallas_call | solution.py:323
  46.4 3.8 %collective-permute-done.6.received_ref = bf16[8,3,128,128]{3,2,1,0:T(8,128)(2,1)S(1)} collective-permute-done((bf16[8,3,128,128]{3,2,1,0:T(8,128)(2,1)}, bf16[8,3,128,128]{3,2,1,0:T(8,128)(2,1)S(1)}, u32[]{:S(2)}, u32[]{:S(2)}) %collective-permute-start.6) | collective-permute-done | bytes 786464 | tf_op jit(solution)/shard_map/ppermute | solution.py:573
  51.7 1.6 collective-permute-start.5
  53.3 6.5 %left.4 = (bf16[8,1,8,256,128]{4,3,2,1,0:T(8,128)(2,1)S(1)}, bf16[8,1,8,256,128]{4,3,2,1,0:T(8,128)(2,1)S(1)}, bf16[8,1,8,256,128]{4,3,2,1,0:T(8,128)(2,1)S(1)}, f32[8,128]{1,0:T(8,128)S(1)}) custom-call(s32[4]{0:T(128)S(1)} %pad_add_fusion.meta, s32[8]{0:T(128)S(1)} %select_reduce_fusion.places, s32[32]{0:T(128)S(1)} %copy-done.13, ...), custom_call_target="tpu_custom_call" | custom-call | flops 9437184 | bytes 8192 | tf_op jit(solution)/shard_map/left/pallas_call | solution.py:257
  59.8 2.0 %copy-done.7 = bf16[8,1,8,256,128]{4,3,2,1,0:T(8,128)(2,1)} copy-done((bf16[8,1,8,256,128]{4,3,2,1,0:T(8,128)(2,1)}, bf16[8,1,8,256,128]{4,3,2,1,0:T(8,128)(2,1)S(1)}, u32[]{:S(2)}) %copy-start.7) | copy-done | bytes 4194328
  61.8 13.0 %collective-permute-done.7.rest_3_ = bf16[2,8,1,128,128]{4,3,2,1,0:T(8,128)(2,1)S(1)} collective-permute-done((bf16[2,8,1,128,128]{4,3,2,1,0:T(8,128)(2,1)S(1)}, bf16[2,8,1,128,128]{4,3,2,1,0:T(8,128)(2,1)S(1)}, u32[]{:S(2)}, u32[]{:S(2)}) %collective-permute-start.7) | collective-permute-done | bytes 524320 | tf_op jit(solution)/shard_map/ppermute | solution.py:573
  76.2 1.4 collective-permute-done.8.received_ref.rest_4_
  77.6 1.5 collective-permute-start.9
  79.2 10.1 %chunk.4 = (f32[8,16,128,128]{3,2,1,0:T(8,128)S(1)}, f32[8,128]{1,0:T(8,128)S(1)}) custom-call(s32[4]{0:T(128)S(1)} %pad_add_fusion.meta, s32[8]{0:T(128)S(1)} %select_reduce_fusion.places, s32[32]{0:T(128)S(1)} %copy-done.13, s32[8,2]{1,0:T(8,128)S(1)} %copy.35.partners, s32[8]{0:T(128)S(1)} %copy-done.12, ...), custom_call_target="tpu_custom_call" | custom-call | flops 13631488 | bytes 8192 | tf_op jit(solution)/shard_map/chunk/pallas_call | solution.py:449
  89.3 13.2 %collective-permute-done.10.rest_3_ = bf16[2,8,1,128,128]{4,3,2,1,0:T(8,128)(2,1)S(1)} collective-permute-done((bf16[2,8,1,128,128]{4,3,2,1,0:T(8,128)(2,1)S(1)}, bf16[2,8,1,128,128]{4,3,2,1,0:T(8,128)(2,1)S(1)}, u32[]{:S(2)}, u32[]{:S(2)}) %collective-permute-start.10) | collective-permute-done | bytes 524320 | tf_op jit(solution)/shard_map/ppermute | solution.py:573
  105.5 1.6 collective-permute-start.12
  107.1 9.2 %chunk.5 = (f32[8,16,128,128]{3,2,1,0:T(8,128)S(1)}, f32[8,128]{1,0:T(8,128)S(1)}) custom-call(s32[4]{0:T(128)S(1)} %pad_add_fusion.meta, s32[8]{0:T(128)S(1)} %select_reduce_fusion.places, s32[32]{0:T(128)S(1)} %copy-done.13, s32[8,2]{1,0:T(8,128)S(1)} %copy.35.partners, s32[8]{0:T(128)S(1)} %copy-done.12, ...), custom_call_target="tpu_custom_call", output_to_operand_aliasing={{0}: (13, {})} | custom-call | flops 10485760 | bytes 8192 | tf_op jit(solution)/shard_map/chunk/pallas_call | solution.py:449
  116.3 5.1 %left.5 = (bf16[8,1,8,256,128]{4,3,2,1,0:T(8,128)(2,1)S(1)}, bf16[8,1,8,256,128]{4,3,2,1,0:T(8,128)(2,1)S(1)}, f32[8,128]{1,0:T(8,128)S(1)}) custom-call(s32[4]{0:T(128)S(1)} %pad_add_fusion.meta, s32[8]{0:T(128)S(1)} %select_reduce_fusion.places, s32[32]{0:T(128)S(1)} %copy-done.13, s32[8,2]{1,0:T(8,128)S(1)} %copy.35.partners, s32[8]{0:T(128)S(1)} %copy-done.12, ...), custom_call_target="tpu_custom_call" | custom-call | flops 6291456 | bytes 8192 | tf_op jit(solution)/shard_map/left/pallas_call | solution.py:257
  121.5 7.7 %collective-permute-done.13.rest_3_ = bf16[2,8,1,128,128]{4,3,2,1,0:T(8,128)(2,1)S(1)} collective-permute-done((bf16[2,8,1,128,128]{4,3,2,1,0:T(8,128)(2,1)S(1)}, bf16[2,8,1,128,128]{4,3,2,1,0:T(8,128)(2,1)S(1)}, u32[]{:S(2)}, u32[]{:S(2)}) %collective-permute-start.13) | collective-permute-done | bytes 524320 | tf_op jit(solution)/shard_map/ppermute | solution.py:573
  130.5 1.5 collective-permute-done.14.received_ref.rest_5_
  132.0 1.5 collective-permute-start.15
  133.5 9.2 %chunk.6 = (f32[8,16,128,128]{3,2,1,0:T(8,128)S(1)}, f32[8,128]{1,0:T(8,128)S(1)}) custom-call(s32[4]{0:T(128)S(1)} %pad_add_fusion.meta, s32[8]{0:T(128)S(1)} %select_reduce_fusion.places, s32[32]{0:T(128)S(1)} %copy-done.13, s32[8,2]{1,0:T(8,128)S(1)} %copy.35.partners, s32[8]{0:T(128)S(1)} %copy-done.12, ...), custom_call_target="tpu_custom_call", output_to_operand_aliasing={{0}: (13, {})} | custom-call | flops 10485760 | bytes 8192 | tf_op jit(solution)/shard_map/chunk/pallas_call | solution.py:449
  142.8 3.2 %collective-permute-done.15.rest_6_ = bf16[2,8,1,128,128]{4,3,2,1,0:T(8,128)(2,1)S(1)} collective-permute-done((bf16[2,8,1,128,128]{4,3,2,1,0:T(8,128)(2,1)S(1)}, bf16[2,8,1,128,128]{4,3,2,1,0:T(8,128)(2,1)S(1)}, u32[]{:S(2)}, u32[]{:S(2)}) %collective-permute-start.15) | collective-permute-done | bytes 524320 | tf_op jit(solution)/shard_map/ppermute | solution.py:573
  146.0 6.3 %chunk.7 = (bf16[8,16,128,128]{3,2,1,0:T(8,128)(2,1)S(1)}, f32[8,128]{1,0:T(8,128)S(1)}) custom-call(s32[4]{0:T(128)S(1)} %pad_add_fusion.meta, s32[8]{0:T(128)S(1)} %select_reduce_fusion.places, s32[32]{0:T(128)S(1)} %copy-done.13, s32[8,2]{1,0:T(8,128)S(1)} %copy.35.partners, s32[8]{0:T(128)S(1)} %copy-done.12, f32[8,128]{1,0:T(8,128)S(1)} %get-tuple-element.65.after_ref, ...), custom_call_target="tpu_custom_call" | custom-call | flops 4194304 | bytes 8192 | tf_op jit(solution)/shard_map/chunk/pallas_call | solution.py:449
  153.0 3.2 %collective-permute-done.16 = f32[16,128]{1,0:T(8,128)S(1)} collective-permute-done((f32[16,128]{1,0:T(8,128)S(1)}, f32[16,128]{1,0:T(8,128)S(1)}, u32[]{:S(2)}, u32[]{:S(2)}) %collective-permute-start.16) | collective-permute-done | bytes 8224 | tf_op jit(solution)/shard_map/ppermute | solution.py:573
  156.2 2.5 %collective-permute-start.17 = (f32[16,128]{1,0:T(8,128)S(1)}, f32[16,128]{1,0:T(8,128)S(1)}, u32[]{:S(2)}, u32[]{:S(2)}) collective-permute-start(f32[16,128]{1,0:T(8,128)S(1)} %add.42), channel_id=1, source_target_pairs={{0,8},{4,12},{8,0},{12,4},{1,9},{5,13},{9,1},{13,5},{2,10},{6,14},... | collective-permute-start | bytes 24584 | tf_op jit(solution)/shard_map/ppermute | solution.py:573
  158.7 2.0 %collective-permute-done.17 = f32[16,128]{1,0:T(8,128)S(1)} collective-permute-done((f32[16,128]{1,0:T(8,128)S(1)}, f32[16,128]{1,0:T(8,128)S(1)}, u32[]{:S(2)}, u32[]{:S(2)}) %collective-permute-start.17) | collective-permute-done | bytes 8224 | tf_op jit(solution)/shard_map/ppermute | solution.py:573
  161.9 6.6 %residual.1 = (bf16[8,2,16,128,128]{4,3,2,1,0:T(8,128)(2,1)}, f32[1]{0:T(128)}) custom-call(s32[4]{0:T(128)S(1)} %pad_add_fusion.meta, s32[8]{0:T(128)S(1)} %select_reduce_fusion.places, s32[32]{0:T(128)S(1)} %copy-done.13, s32[8,2]{1,0:T(8,128)S(1)} %copy.35.partners, s32[8]{0:T(128)S(1)} %copy-done.12, f32[16,128]{1,0:T(8,128)S(1)} %add.44.folds_ref, ...), custom_call_target="tpu_custom_call" | custom-call | flops 12582912 | bytes 25165824 | tf_op jit(solution)/shard_map/residual/pallas_call | solution.py:527
  (73 shorter events, 15.4 us)
Async XLA Ops:
  0.6 24.9 %copy-start.12 = (s32[8]{0:T(128)S(1)}, s32[8]{0:T(128)}, u32[]{:S(2)}) copy-start(s32[8]{0:T(128)} %counts.15) | copy-start | bytes 100
  0.6 24.9 %copy-start.13 = (s32[32]{0:T(128)S(1)}, s32[32]{0:T(128)}, u32[]{:S(2)}) copy-start(s32[32]{0:T(128)} %sector_rows.15) | copy-start | bytes 388
  0.7 24.7 %copy-start.14 = (s32[8,2]{0,1:T(2,128)S(1)}, s32[8,2]{0,1:T(2,128)}, u32[]{:S(2)}) copy-start(s32[8,2]{0,1:T(2,128)} %param.14) | copy-start | bytes 196
  6.3 16.4 %collective-permute-start = (bf16[2112,128]{1,0:T(8,128)(2,1)}, bf16[2112,128]{1,0:T(8,128)(2,1)S(1)}, u32[]{:S(2)}, u32[]{:S(2)}) collective-permute-start(bf16[2112,128]{1,0:T(8,128)(2,1)} %get-tuple-element.39), channel_id=1, source_target_pairs={{0,1},{1,0},{2,3},{3,2},{4,5},{5,4},{6,7},{7,6},{8,9},{9,8},{10,11... | collective-permute-start | bytes 1622024 | tf_op jit(solution)/shard_map/ppermute | solution.py:573
  6.8 9.8 %collective-permute-start.1 = (bf16[8,1,128,128]{3,2,1,0:T(8,128)(2,1)}, bf16[8,1,128,128]{3,2,1,0:T(8,128)(2,1)S(1)}, u32[]{:S(2)}, u32[]{:S(2)}) collective-permute-start(bf16[8,1,128,128]{3,2,1,0:T(8,128)(2,1)} %get-tuple-element.41.near_ref), channel_id=1, source_target_pairs={{0,4},{4,0},{8,12},{12,8},{1,5},{5,1},{9,13},{13,9},{2,6},{6,2},{1... | collective-permute-start | bytes 786440 | tf_op jit(solution)/shard_map/ppermute | solution.py:573
  18.3 26.2 %collective-permute-start.2 = (bf16[2,8,1,128,128]{4,3,2,1,0:T(8,128)(2,1)}, bf16[2,8,1,128,128]{4,3,2,1,0:T(8,128)(2,1)}, u32[]{:S(2)}, u32[]{:S(2)}) collective-permute-start(bf16[2,8,1,128,128]{4,3,2,1,0:T(8,128)(2,1)} %stack.30.rest_1_), channel_id=1, source_target_pairs={{0,8},{4,12},{8,0},{12,4},{1,9},{5,13},{9,1},{13,5},{2,10},{6,14},... | collective-permute-start | bytes 1572872 | tf_op jit(solution)/shard_map/ppermute | solution.py:573
  21.1 29.2 %collective-permute-start.6 = (bf16[8,3,128,128]{3,2,1,0:T(8,128)(2,1)}, bf16[8,3,128,128]{3,2,1,0:T(8,128)(2,1)S(1)}, u32[]{:S(2)}, u32[]{:S(2)}) collective-permute-start(bf16[8,3,128,128]{3,2,1,0:T(8,128)(2,1)} %get-tuple-element.46.near_ref), channel_id=1, source_target_pairs={{0,4},{4,0},{8,12},{12,8},{1,5},{5,1},{9,13},{13,9},{2,6},{6,2},{1... | collective-permute-start | bytes 2359304 | tf_op jit(solution)/shard_map/ppermute | solution.py:573
  23.8 29.5 %collective-permute-start.4 = (bf16[2,2112,128]{2,1,0:T(8,128)(2,1)S(1)}, bf16[2,2112,128]{2,1,0:T(8,128)(2,1)S(1)}, u32[]{:S(2)}, u32[]{:S(2)}) collective-permute-start(bf16[2,2112,128]{2,1,0:T(8,128)(2,1)S(1)} %stack.29.rest_0_), channel_id=1, source_target_pairs={{0,2},{1,3},{2,0},{3,1},{4,6},{5,7},{6,4},{7,5},{8,10},{9,11},{10,... | collective-permute-start | bytes 3244040 | tf_op jit(solution)/shard_map/ppermute | solution.py:573
  26.6 23.7 %copy-start = (bf16[8,3,128,128]{3,2,1,0:T(8,128)(2,1)S(1)}, bf16[8,3,128,128]{3,2,1,0:T(8,128)(2,1)}, u32[]{:S(2)}) copy-start(bf16[8,3,128,128]{3,2,1,0:T(8,128)(2,1)} %get-tuple-element.46.near_ref) | copy-start | bytes 2359300
  36.2 2.0 %copy-start.3 = (bf16[8,1,8,256,128]{4,3,2,1,0:T(8,128)(2,1)}, bf16[8,1,8,256,128]{4,3,2,1,0:T(8,128)(2,1)S(1)}, u32[]{:S(2)}) copy-start(bf16[8,1,8,256,128]{4,3,2,1,0:T(8,128)(2,1)S(1)} %get-tuple-element.49.rest_0_) | copy-start | bytes 12582916
  38.2 21.6 %copy-start.1 = (bf16[8,1,8,256,128]{4,3,2,1,0:T(8,128)(2,1)}, bf16[8,1,8,256,128]{4,3,2,1,0:T(8,128)(2,1)S(1)}, u32[]{:S(2)}) copy-start(bf16[8,1,8,256,128]{4,3,2,1,0:T(8,128)(2,1)S(1)} %get-tuple-element.54.rest_0_) | copy-start | bytes 12582916
  38.2 21.6 %copy-start.5 = (bf16[8,1,8,256,128]{4,3,2,1,0:T(8,128)(2,1)}, bf16[8,1,8,256,128]{4,3,2,1,0:T(8,128)(2,1)S(1)}, u32[]{:S(2)}) copy-start(bf16[8,1,8,256,128]{4,3,2,1,0:T(8,128)(2,1)S(1)} %get-tuple-element.66.rest_0_) | copy-start | bytes 12582916
  46.3 5.3 %collective-permute-start.3 = (bf16[8,1,128,128]{3,2,1,0:T(8,128)(2,1)S(1)}, bf16[8,1,128,128]{3,2,1,0:T(8,128)(2,1)S(1)}, u32[]{:S(2)}, u32[]{:S(2)}) collective-permute-start(bf16[8,1,128,128]{3,2,1,0:T(8,128)(2,1)S(1)} %get-tuple-element.43), channel_id=1, source_target_pairs={{0,1},{1,0},{2,3},{3,2},{4,5},{5,4},{6,7},{7,6},{8,9},{9,8},{10,11... | collective-permute-start | bytes 786440 | tf_op jit(solution)/shard_map/ppermute | solution.py:573
  50.3 24.5 %collective-permute-start.7 = (bf16[2,8,1,128,128]{4,3,2,1,0:T(8,128)(2,1)S(1)}, bf16[2,8,1,128,128]{4,3,2,1,0:T(8,128)(2,1)S(1)}, u32[]{:S(2)}, u32[]{:S(2)}) collective-permute-start(bf16[2,8,1,128,128]{4,3,2,1,0:T(8,128)(2,1)S(1)} %stack.32.rest_2_), channel_id=1, source_target_pairs={{0,8},{4,12},{8,0},{12,4},{1,9},{5,13},{9,1},{13,5},{2,10},{6,14},... | collective-permute-start | bytes 1572872 | tf_op jit(solution)/shard_map/ppermute | solution.py:573
  51.7 23.1 %collective-permute-start.5 = (bf16[2,8,1,128,128]{4,3,2,1,0:T(8,128)(2,1)S(1)}, bf16[2,8,1,128,128]{4,3,2,1,0:T(8,128)(2,1)S(1)}, u32[]{:S(2)}, u32[]{:S(2)}) collective-permute-start(bf16[2,8,1,128,128]{4,3,2,1,0:T(8,128)(2,1)S(1)} %stack.31.rest_0_), channel_id=1, source_target_pairs={{0,2},{1,3},{2,0},{3,1},{4,6},{5,7},{6,4},{7,5},{8,10},{9,11},{10,... | collective-permute-start | bytes 1572872 | tf_op jit(solution)/shard_map/ppermute | solution.py:573
  59.8 2.0 %copy-start.7 = (bf16[8,1,8,256,128]{4,3,2,1,0:T(8,128)(2,1)}, bf16[8,1,8,256,128]{4,3,2,1,0:T(8,128)(2,1)S(1)}, u32[]{:S(2)}) copy-start(bf16[8,1,8,256,128]{4,3,2,1,0:T(8,128)(2,1)S(1)} %get-tuple-element.67.rest_1_) | copy-start | bytes 12582916
  61.8 17.3 %copy-start.4 = (bf16[8,1,8,256,128]{4,3,2,1,0:T(8,128)(2,1)S(1)}, bf16[8,1,8,256,128]{4,3,2,1,0:T(8,128)(2,1)}, u32[]{:S(2)}) copy-start(bf16[8,1,8,256,128]{4,3,2,1,0:T(8,128)(2,1)} %copy-done.3) | copy-start | bytes 12582916
  76.0 1.6 collective-permute-start.8
  76.1 26.4 %collective-permute-start.10 = (bf16[2,8,1,128,128]{4,3,2,1,0:T(8,128)(2,1)S(1)}, bf16[2,8,1,128,128]{4,3,2,1,0:T(8,128)(2,1)S(1)}, u32[]{:S(2)}, u32[]{:S(2)}) collective-permute-start(bf16[2,8,1,128,128]{4,3,2,1,0:T(8,128)(2,1)S(1)} %stack.34.rest_2_), channel_id=1, source_target_pairs={{0,8},{4,12},{8,0},{12,4},{1,9},{5,13},{9,1},{13,5},{2,10},{6,14},... | collective-permute-start | bytes 1572872 | tf_op jit(solution)/shard_map/ppermute | solution.py:573
  77.6 24.9 %collective-permute-start.9 = (bf16[2,8,1,128,128]{4,3,2,1,0:T(8,128)(2,1)S(1)}, bf16[2,8,1,128,128]{4,3,2,1,0:T(8,128)(2,1)S(1)}, u32[]{:S(2)}, u32[]{:S(2)}) collective-permute-start(bf16[2,8,1,128,128]{4,3,2,1,0:T(8,128)(2,1)S(1)} %stack.33.after_ref), channel_id=1, source_target_pairs={{0,2},{1,3},{2,0},{3,1},{4,6},{5,7},{6,4},{7,5},{8,10},{9,11},{10,... | collective-permute-start | bytes 1572872 | tf_op jit(solution)/shard_map/ppermute | solution.py:573
  89.3 17.8 %copy-start.2 = (bf16[8,1,8,256,128]{4,3,2,1,0:T(8,128)(2,1)S(1)}, bf16[8,1,8,256,128]{4,3,2,1,0:T(8,128)(2,1)}, u32[]{:S(2)}) copy-start(bf16[8,1,8,256,128]{4,3,2,1,0:T(8,128)(2,1)} %copy-done.1) | copy-start | bytes 12582916
  103.9 1.6 collective-permute-start.11
  104.0 25.1 %collective-permute-start.13 = (bf16[2,8,1,128,128]{4,3,2,1,0:T(8,128)(2,1)S(1)}, bf16[2,8,1,128,128]{4,3,2,1,0:T(8,128)(2,1)S(1)}, u32[]{:S(2)}, u32[]{:S(2)}) collective-permute-start(bf16[2,8,1,128,128]{4,3,2,1,0:T(8,128)(2,1)S(1)} %stack.36.rest_2_), channel_id=1, source_target_pairs={{0,8},{4,12},{8,0},{12,4},{1,9},{5,13},{9,1},{13,5},{2,10},{6,14},... | collective-permute-start | bytes 1572872 | tf_op jit(solution)/shard_map/ppermute | solution.py:573
  105.5 23.7 %collective-permute-start.12 = (bf16[2,8,1,128,128]{4,3,2,1,0:T(8,128)(2,1)S(1)}, bf16[2,8,1,128,128]{4,3,2,1,0:T(8,128)(2,1)S(1)}, u32[]{:S(2)}, u32[]{:S(2)}) collective-permute-start(bf16[2,8,1,128,128]{4,3,2,1,0:T(8,128)(2,1)S(1)} %stack.35.after_ref), channel_id=1, source_target_pairs={{0,2},{1,3},{2,0},{3,1},{4,6},{5,7},{6,4},{7,5},{8,10},{9,11},{10,... | collective-permute-start | bytes 1572872 | tf_op jit(solution)/shard_map/ppermute | solution.py:573
  130.3 1.6 collective-permute-start.14
  132.0 14.0 %collective-permute-start.15 = (bf16[2,8,1,128,128]{4,3,2,1,0:T(8,128)(2,1)S(1)}, bf16[2,8,1,128,128]{4,3,2,1,0:T(8,128)(2,1)S(1)}, u32[]{:S(2)}, u32[]{:S(2)}) collective-permute-start(bf16[2,8,1,128,128]{4,3,2,1,0:T(8,128)(2,1)S(1)} %stack.37.after_ref), channel_id=1, source_target_pairs={{0,2},{1,3},{2,0},{3,1},{4,6},{5,7},{6,4},{7,5},{8,10},{9,11},{10,... | collective-permute-start | bytes 1572872 | tf_op jit(solution)/shard_map/ppermute | solution.py:573
  133.5 12.5 %copy-start.6 = (bf16[8,1,8,256,128]{4,3,2,1,0:T(8,128)(2,1)S(1)}, bf16[8,1,8,256,128]{4,3,2,1,0:T(8,128)(2,1)}, u32[]{:S(2)}) copy-start(bf16[8,1,8,256,128]{4,3,2,1,0:T(8,128)(2,1)} %copy-done.5) | copy-start | bytes 12582916
  133.5 12.5 %copy-start.8 = (bf16[8,1,8,256,128]{4,3,2,1,0:T(8,128)(2,1)S(1)}, bf16[8,1,8,256,128]{4,3,2,1,0:T(8,128)(2,1)}, u32[]{:S(2)}) copy-start(bf16[8,1,8,256,128]{4,3,2,1,0:T(8,128)(2,1)} %copy-done.7) | copy-start | bytes 12582916
  152.4 9.6 %collective-permute-start.19 = (bf16[8,16,128,128]{3,2,1,0:T(8,128)(2,1)S(1)}, bf16[8,16,128,128]{3,2,1,0:T(8,128)(2,1)S(1)}, u32[]{:S(2)}, u32[]{:S(2)}) collective-permute-start(bf16[8,16,128,128]{3,2,1,0:T(8,128)(2,1)S(1)} %get-tuple-element.73.own_ref), channel_id=1, source_target_pairs={{0,1},{1,0},{2,3},{3,2},{4,5},{5,4},{6,7},{7,6},{8,9},{9,8},{10,11... | collective-permute-start | bytes 12582920 | tf_op jit(solution)/shard_map/ppermute | solution.py:573
  152.5 3.7 %collective-permute-start.16 = (f32[16,128]{1,0:T(8,128)S(1)}, f32[16,128]{1,0:T(8,128)S(1)}, u32[]{:S(2)}, u32[]{:S(2)}) collective-permute-start(f32[16,128]{1,0:T(8,128)S(1)} %constant_dynamic-update-slice_fusion), channel_id=1, source_target_pairs={{0,4},{4,0},{8,12},{12,8},{1,5},{5,1},{9,13},{13,9},{2,6},{6,2},{1... | collective-permute-start | bytes 24584 | tf_op jit(solution)/shard_map/ppermute | solution.py:573
  156.2 4.5 %collective-permute-start.17 = (f32[16,128]{1,0:T(8,128)S(1)}, f32[16,128]{1,0:T(8,128)S(1)}, u32[]{:S(2)}, u32[]{:S(2)}) collective-permute-start(f32[16,128]{1,0:T(8,128)S(1)} %add.42), channel_id=1, source_target_pairs={{0,8},{4,12},{8,0},{12,4},{1,9},{5,13},{9,1},{13,5},{2,10},{6,14},... | collective-permute-start | bytes 24584 | tf_op jit(solution)/shard_map/ppermute | solution.py:573
  160.7 1.2 collective-permute-start.18
  (3 other events, 3.0 us)
